TPU v7x, 1024 devices: a whole 4x4x32 slice. The times are simulated.
1024 devices in a mesh: group: 64 (over z, core), slot: 16 (over y, x).
Axes of the slice: x: 4, y: 4, z: 32, core: 2. Of those that a mesh axis runs over, the one named last changes fastest.
Arguments:
- tokens: bfloat16 [8192, 7168], P('group', 'slot'), may hold values from -620 to 620, as said below
- norm_gain: float32 [7168], P('slot'), may hold values from 0.1 to 1.9
- route_expert: int32 [8192, 2], P('group'), may hold values from 0 to 63, all different within a row; in each aligned block of 128 rows (0 to 127, 128 to 255, ...) at most 8 rows name the same one
- route_gate: bfloat16 [8192, 2], P('group'), may hold values from 0.29882812 to 2.5
- w_gate_up: bfloat16 [64, 7168, 2048], P('group', 'slot'), may hold values from -0.0625 to 0.0625
- w_down: bfloat16 [64, 1024, 7168], P('group', None, 'slot'), may hold values from -0.1875 to 0.1875
Outputs:
- mixed: bfloat16 [8192, 7168], P('group', 'slot')
Inputs may be any that keep to these rules, and one draw needn't show every extreme that they name: `route_expert`: in the 128 rows of one group block no expert is named more than 8 times, a bound that some block reaches; a token's 2 experts differ. `tokens`: token rows; every row and column of order one up to a scale.
All inputs are finite; a program needn't handle non-finite values.
Results may differ from a plain program's by a relative error of at most 0.029.
Values may be sent and summed in bfloat16 or wider, within the bound.
No kernel may reach another device: no remote copies, remote signals or barrier semaphores. Data moves between devices by JAX's collectives and lax.ppermute only.
A program may use at most 32 MiB of HBM per device.

v0:
```python
import jax
import jax.numpy as jnp
from jax import lax
from jax.sharding import PartitionSpec as P

D = 7168


NORM_EPS = 1e-06


def expert_rows(arrived, w_gate_up, w_down):
    inner = w_gate_up.shape[2] // 2
    mine = lax.psum_scatter(
        jnp.dot(arrived, w_gate_up[0], preferred_element_type=jnp.float32).astype(jnp.bfloat16),
        "slot",
        scatter_dimension=0,
        tiled=True,
    ).astype(jnp.float32)
    hidden = (jax.nn.silu(mine[:, :inner]) * mine[:, inner:]).astype(jnp.bfloat16)
    result = jnp.dot(
        lax.all_gather(hidden, "slot", axis=0, tiled=True),
        w_down[0],
        preferred_element_type=jnp.float32,
    )
    return result.astype(jnp.bfloat16)


def local(tokens, norm_gain, route_expert, route_gate, w_gate_up, w_down):
    tok_rows, width = tokens.shape
    groups = lax.axis_size("group")
    picks = route_expert.shape[1]
    capacity = 2 * tok_rows * picks // groups
    slots = groups * capacity
    values = tokens.astype(jnp.float32)
    squares = lax.psum(jnp.sum(values * values, axis=1), "slot")
    normed = (values * lax.rsqrt(squares / D + NORM_EPS)[:, None] * norm_gain[None, :]).astype(
        jnp.bfloat16
    )
    flat_routes = route_expert.reshape(-1)
    chosen = (flat_routes[:, None] == jnp.arange(groups, dtype=jnp.int32)[None, :]).astype(
        jnp.int32
    )
    before = jnp.cumsum(chosen, axis=0) - chosen
    place = jnp.sum(before * chosen, axis=1)
    target = flat_routes * capacity + place
    picked = (target[:, None] == jnp.arange(slots, dtype=jnp.int32)[None, :]).reshape(
        tok_rows, picks, slots
    )
    spread = jnp.sum(picked.astype(jnp.float32), axis=1).astype(jnp.bfloat16)
    weights_back = jnp.sum(
        picked.astype(jnp.float32) * route_gate.astype(jnp.float32)[:, :, None], axis=1
    ).astype(jnp.bfloat16)
    outgoing = jnp.einsum("tr,td->rd", spread, normed, preferred_element_type=jnp.float32)
    outgoing = outgoing.astype(jnp.bfloat16).reshape(groups, capacity, width)
    arrived = lax.all_to_all(outgoing, "group", split_axis=0, concat_axis=0, tiled=True)
    finished = expert_rows(arrived.reshape(slots, width), w_gate_up, w_down).reshape(
        groups, capacity, width
    )
    returned = lax.all_to_all(finished, "group", split_axis=0, concat_axis=0, tiled=True)
    mixed = jnp.dot(
        weights_back, returned.reshape(slots, width), preferred_element_type=jnp.float32
    )
    return mixed.astype(jnp.bfloat16)


def solution(mesh):
    placed = (
        P("group", "slot"),
        P("slot"),
        P("group", None),
        P("group", None),
        P("group", "slot", None),
        P("group", None, "slot"),
    )
    return jax.shard_map(
        local, mesh=mesh, in_specs=placed, out_specs=P("group", "slot"), check_vma=False
    )
```

profile of v0, /device:TPU:6, one launch (start us, length us, event | category | flops | bytes accessed | tf_op | source)
XLA Modules:
  0.0 419.3 jit_solution(10710699166060006557)
XLA Ops:
  6.5 0.9 copy.25
  7.5 0.1 eq.43
  7.6 0.1 eq.39
  7.7 1.0 fusion.4
  8.7 44.6 %psum.7 = f32[128]{0:T(128)S(1)} all-reduce(f32[128]{0:T(128)S(1)} %fusion.4), channel_id=1, replica_groups=mesh['group'=64,'slot'=16] {'slot'}, use_global_device_ids=true, to_apply=%region_6.7 | all-reduce | flops 128 | bytes 1024 | tf_op jit(solution)/shard_map/psum | solution.py:36
  53.4 0.7 convert_element_type.46
  54.0 0.6 reduce-window.6
  54.6 0.2 slice_reduce_fusion
  54.9 0.1 fusion.15
  55.0 0.1 reduce_sum.39
  55.2 0.7 multiply_add_fusion
  55.9 0.2 select_reduce_fusion
  56.1 1.2 convolution_convert_fusion.1
  57.3 0.2 copy.29
  57.5 83.0 %all_to_all.10 = bf16[64,8,448]{2,1,0:T(8,128)(2,1)S(1)} all-to-all(bf16[64,8,448]{2,1,0:T(8,128)(2,1)S(1)} %bitcast.36), channel_id=1, replica_groups=mesh['group'=64,'slot'=16] {'group'}, dimensions={0} | all-to-all | bytes 917504 | tf_op jit(solution)/shard_map/all_to_all | solution.py:56
  140.5 2.6 convolution_convert_fusion
  143.2 94.1 %reduce-scatter.2.cloned.1.call-done = bf16[32,2048]{1,0:T(8,128)(2,1)} async-done(((bf16[512,2048]{1,0:T(8,128)(2,1)}), bf16[32,2048]{1,0:T(8,128)(2,1)}) %reduce-scatter.2.cloned.1.call-update) | async-done | bytes 131088 | tf_op jit(solution)/shard_map/reduce_scatter | solution.py:14
  237.3 0.9 convert_element_type.54
  238.2 0.7 fusion.7
  238.9 81.1 %all-gather.2.cloned.1.call-done = bf16[512,1024]{1,0:T(8,128)(2,1)} async-done(((bf16[32,1024]{1,0:T(8,128)(2,1)}), bf16[512,1024]{1,0:T(8,128)(2,1)}) %all-gather.2.cloned.1.call-update) | async-done | bytes 1048592 | tf_op jit(solution)/shard_map/all_gather | solution.py:22
  320.0 2.2 convolution_convert_fusion.2
  322.1 0.2 copy.30
  322.4 89.1 %all_to_all.11 = bf16[64,8,448]{2,1,0:T(8,128)(2,1)S(1)} all-to-all(bf16[64,8,448]{2,1,0:T(8,128)(2,1)S(1)} %bitcast.37), channel_id=1, replica_groups=mesh['group'=64,'slot'=16] {'group'}, dimensions={0} | all-to-all | bytes 917504 | tf_op jit(solution)/shard_map/all_to_all | solution.py:60
  411.4 1.0 convolution_convert_fusion.3
  (11 shorter events, 0.2 us)
Async XLA Ops:
  6.5 133.9 %copy-start = (bf16[1,448,2048]{2,1,0:T(8,128)(2,1)S(1)}, bf16[1,448,2048]{2,1,0:T(8,128)(2,1)}, u32[]{:S(2)}) copy-start(bf16[1,448,2048]{2,1,0:T(8,128)(2,1)} %param.10) | copy-start | bytes 5505028
  6.5 230.7 %reduce-scatter.2.cloned.1.call-start = ((), (), s32[]{:S(2)}) async-start(), calls=%async_computation.3 | async-start | bytes 2228224 | tf_op jit(solution)/shard_map/reduce_scatter | solution.py:14
  143.1 176.8 %all-gather.2.cloned.1.call-start = ((), (), s32[]{:S(2)}) async-start(), calls=%async_computation.4 | async-start | bytes 1114112 | tf_op jit(solution)/shard_map/all_gather | solution.py:22
Sparse Core Ops, SparseCore 0:
  143.2 93.9 reduce-scatter.1
  242.2 77.7 all-gather.1
where the time goes:
time: 420 us; the launch traced here: 419 us
  blocking collectives  217 us (52%)
  waiting for transfers between devices  175 us (42%)
  between operations  13.5 us (3%)
  matrix products  7.01 us (2%)
  other arithmetic  4.88 us (1%)
    reduce_scatter x1, waiting for transfers between devices, expert_rows(): lax.psum_scatter(jnp.dot(arrived, w_gate_up[0], preferred_element_type=jn...  94.1 us
    all_to_all x1, blocking collectives, local(): lax.all_to_all(finished, 'group', split_axis=0, concat_axis=0, tiled=True)  89.1 us
    all_to_all x1, blocking collectives, local(): lax.all_to_all(outgoing, 'group', split_axis=0, concat_axis=0, tiled=True)  83 us
    all_gather x1, waiting for transfers between devices, expert_rows(): lax.all_gather(hidden, 'slot', axis=0, tiled=True)  81.1 us
    psum x1, blocking collectives, local(): squares = lax.psum(jnp.sum(values * values, axis=1), 'slot')  44.6 us
  transfers between devices with their start and end apart: 2, of which 2 were waited for; matrix products, arithmetic and copies ran while one was open for 0% of the time, Pallas kernels for 0%

commit v1 on v0

v1 whole, which is shorter than its diff:
```python
import jax
import jax.numpy as jnp
from jax import lax
from jax.sharding import PartitionSpec as P

D = 7168


NORM_EPS = 1e-06
LANES = 128


def split_rows(values):
    high = lax.reduce_precision(values, 8, 7)
    low = values - high
    column = jnp.arange(LANES, dtype=jnp.int32)[None, :]
    block = jnp.where(column == 0, high[:, None], jnp.where(column == 1, low[:, None], 0.0))
    return block.astype(jnp.bfloat16)


def expert_rows(arrived, norm_gain, w_gate_up, w_down):
    slots = arrived.shape[0]
    ways = lax.axis_size("slot")
    both = w_gate_up.shape[2]
    inner = both // 2
    every = [list(range(ways))]
    values = arrived.astype(jnp.float32)
    squares = jnp.sum(values * values, axis=1)
    gained = (values * norm_gain[None, :]).astype(jnp.bfloat16)
    partial = jnp.dot(gained, w_gate_up[0], preferred_element_type=jnp.float32).astype(jnp.bfloat16)
    sent = jnp.concatenate([partial, split_rows(squares)], axis=1)
    pieces = lax.all_to_all(
        sent.reshape(ways, slots // ways, both + LANES),
        "slot",
        split_axis=0,
        concat_axis=0,
        tiled=True,
        axis_index_groups=every,
    )
    mine = jnp.sum(pieces.astype(jnp.float32), axis=0)
    scale = lax.rsqrt((mine[:, both : both + 1] + mine[:, both + 1 : both + 2]) / D + NORM_EPS)
    gate, up = mine[:, :inner] * scale, mine[:, inner:both] * scale
    hidden = (jax.nn.silu(gate) * up).astype(jnp.bfloat16)
    spread = lax.all_to_all(
        jnp.broadcast_to(hidden[None], (ways,) + hidden.shape),
        "slot",
        split_axis=0,
        concat_axis=0,
        tiled=True,
        axis_index_groups=every,
    )
    result = jnp.dot(spread.reshape(slots, inner), w_down[0], preferred_element_type=jnp.float32)
    return result.astype(jnp.bfloat16)


def local(tokens, norm_gain, route_expert, route_gate, w_gate_up, w_down):
    tok_rows, width = tokens.shape
    groups = lax.axis_size("group")
    picks = route_expert.shape[1]
    capacity = 2 * tok_rows * picks // groups
    slots = groups * capacity
    flat_routes = route_expert.reshape(-1)
    chosen = (flat_routes[:, None] == jnp.arange(groups, dtype=jnp.int32)[None, :]).astype(
        jnp.int32
    )
    before = jnp.cumsum(chosen, axis=0) - chosen
    place = jnp.sum(before * chosen, axis=1)
    target = flat_routes * capacity + place
    picked = (target[:, None] == jnp.arange(slots, dtype=jnp.int32)[None, :]).reshape(
        tok_rows, picks, slots
    )
    spread = jnp.sum(picked.astype(jnp.float32), axis=1).astype(jnp.bfloat16)
    weights_back = jnp.sum(
        picked.astype(jnp.float32) * route_gate.astype(jnp.float32)[:, :, None], axis=1
    ).astype(jnp.bfloat16)
    outgoing = jnp.einsum("tr,td->rd", spread, tokens, preferred_element_type=jnp.float32)
    outgoing = outgoing.astype(jnp.bfloat16).reshape(groups, capacity, width)
    arrived = lax.all_to_all(outgoing, "group", split_axis=0, concat_axis=0, tiled=True)
    finished = expert_rows(
        arrived.reshape(slots, width), norm_gain, w_gate_up, w_down
    ).reshape(groups, capacity, width)
    returned = lax.all_to_all(finished, "group", split_axis=0, concat_axis=0, tiled=True)
    mixed = jnp.dot(
        weights_back, returned.reshape(slots, width), preferred_element_type=jnp.float32
    )
    return mixed.astype(jnp.bfloat16)


def solution(mesh):
    placed = (
        P("group", "slot"),
        P("slot"),
        P("group", None),
        P("group", None),
        P("group", "slot", None),
        P("group", None, "slot"),
    )
    return jax.shard_map(
        local, mesh=mesh, in_specs=placed, out_specs=P("group", "slot"), check_vma=False
    )
```

time: 420 us -> 231 us (0.55)
  waiting for transfers between devices: 175 us -> 65.7 us
  blocking collectives: 217 us -> 123 us
  starting transfers between devices: 0.04 us -> 29.3 us
  between operations: 13.5 us -> 0.14 us
    reduce_scatter x1 -> x0, waiting for transfers between devices: 94.1 us -> none  [expert_rows(): lax.psum_scatter(jnp.dot(arrived, w_gate_up[0], preferred_element_type=jn...]
    all_gather x1 -> x0, waiting for transfers between devices: 81.1 us -> none  [expert_rows(): lax.all_gather(hidden, 'slot', axis=0, tiled=True)]
    all_to_all x0 -> x1, waiting for transfers between devices: none -> 65.7 us  [local(): lax.all_to_all(outgoing, 'group', split_axis=0, concat_axis=0, tiled=True)]
    psum x1 -> x0, blocking collectives: 44.6 us -> none  [local(): squares = lax.psum(jnp.sum(values * values, axis=1), 'slot')]
    all_to_all x1 -> x2, blocking collectives: 83 us -> 51.5 us  [the longest x1 34.1 us: expert_rows(): lax.all_to_all(sent.reshape(ways, slots // ways, both + LANES), 'slot', s...]
    all_to_all x0 -> x1, starting transfers between devices: none -> 29.3 us  [local(): lax.all_to_all(outgoing, 'group', split_axis=0, concat_axis=0, tiled=True)]
    all_to_all x1, blocking collectives: 89.1 us -> 71.2 us  [local(): lax.all_to_all(finished, 'group', split_axis=0, concat_axis=0, tiled=True)]
  transfers between devices with their start and end apart: 2 -> 1, of which waited for: 2 -> 1; matrix products, arithmetic and copies ran while one was open for 0% -> 0% of each run, Pallas kernels for 0% -> 0%
where the time goes in v1:
time: 231 us; the launch traced here: 229 us
  blocking collectives  123 us (53%)
  waiting for transfers between devices  65.7 us (28%)
  starting transfers between devices  29.3 us (13%)
  matrix products  4.09 us (2%)
  other arithmetic  3.51 us (2%)
  local copies, waits for them, and re-layouts  3.01 us (1%)
    all_to_all x1, blocking collectives, local(): lax.all_to_all(finished, 'group', split_axis=0, concat_axis=0, tiled=True)  71.2 us
    all_to_all x1, waiting for transfers between devices, local(): lax.all_to_all(outgoing, 'group', split_axis=0, concat_axis=0, tiled=True)  65.7 us
    all_to_all x1, blocking collectives, expert_rows(): lax.all_to_all(sent.reshape(ways, slots // ways, both + LANES), 'slot', s...  34.1 us
    all_to_all x1, starting transfers between devices, local(): lax.all_to_all(outgoing, 'group', split_axis=0, concat_axis=0, tiled=True)  29.3 us
    all_to_all x1, blocking collectives, expert_rows(): lax.all_to_all(jnp.broadcast_to(hidden[None], (ways,) + hidden.shape), 's...  17.4 us
  transfers between devices with their start and end apart: 1, of which 1 were waited for; matrix products, arithmetic and copies ran while one was open for 0% of the time, Pallas kernels for 0%

profile of v1, /device:TPU:6, one launch (start us, length us, event | category | flops | bytes accessed | tf_op | source)
XLA Modules:
  0.0 228.6 jit_solution(6326920946643278480)
XLA Ops:
  0.0 0.9 copy.43
  1.1 0.1 eq.61
  1.2 0.7 convert_element_type.54
  1.9 0.6 reduce-window.6
  2.5 0.2 slice_reduce_fusion
  2.8 0.1 reduce_sum.50
  3.0 0.7 multiply_add_fusion
  3.7 0.2 select_reduce_fusion
  3.9 1.2 convolution_convert_fusion.1
  5.1 1.0 copy.47
  6.1 29.3 %all-to-all-start = ((bf16[64,8,448]{2,1,0:T(8,128)(2,1)}), bf16[64,8,448]{2,1,0:T(8,128)(2,1)S(1)}, u32[]{:S(2)}, u32[]{:S(2)}) async-start(bf16[64,8,448]{2,1,0:T(8,128)(2,1)} %bitcast.1), calls=%async_computation | async-start | bytes 1048576 | tf_op jit(solution)/shard_map/all_to_all | solution.py:78
  35.4 65.7 %all-to-all-done = bf16[64,8,448]{2,1,0:T(8,128)(2,1)S(1)} async-done(((bf16[64,8,448]{2,1,0:T(8,128)(2,1)}), bf16[64,8,448]{2,1,0:T(8,128)(2,1)S(1)}, u32[]{:S(2)}, u32[]{:S(2)}) %all-to-all-start) | async-done | bytes 458784 | tf_op jit(solution)/shard_map/all_to_all | solution.py:78
  101.2 0.2 fusion.2
  101.5 0.2 select_convert_fusion
  101.7 1.3 convolution_convert_fusion
  103.0 0.2 pad_maximum_fusion
  103.2 34.1 %all_to_all.20 = bf16[16,32,2176]{2,1,0:T(8,128)(2,1)S(1)} all-to-all(bf16[16,32,2176]{2,1,0:T(8,128)(2,1)S(1)} %bitcast.39), channel_id=1, replica_groups={{0,1,2,3,4,5,6,7,8,9,10,11,12,13,14,15},{16,17,18,19,20,21,22,23,24,25,..., dimensions={0} | all-to-all | bytes 4456448 | tf_op jit(solution)/shard_map/all_to_all | solution.py:32
  137.3 0.3 convert_reduce_fusion
  137.6 0.2 fusion.19
  138.1 17.4 %all_to_all.21 = bf16[16,32,1024]{2,1,0:T(8,128)(2,1)S(1)} all-to-all(bf16[16,32,1024]{2,1,0:T(8,128)(2,1)S(1)} %broadcast_in_dim.55), channel_id=1, replica_groups={{0,1,2,3,4,5,6,7,8,9,10,11,12,13,14,15},{16,17,18,19,20,21,22,23,24,25,..., dimensions={0} | all-to-all | bytes 2097152 | tf_op jit(solution)/shard_map/all_to_all | solution.py:44
  155.5 0.7 convolution_convert_fusion.2
  156.2 0.2 copy.48
  156.4 71.2 %all_to_all.22 = bf16[64,8,448]{2,1,0:T(8,128)(2,1)S(1)} all-to-all(bf16[64,8,448]{2,1,0:T(8,128)(2,1)S(1)} %bitcast.40), channel_id=1, replica_groups=mesh['group'=64,'slot'=16] {'group'}, dimensions={0} | all-to-all | bytes 917504 | tf_op jit(solution)/shard_map/all_to_all | solution.py:82
  227.6 1.0 convolution_convert_fusion.3
  (17 shorter events, 0.7 us)
Async XLA Ops:
  0.0 101.7 %copy-start = (bf16[1,448,2048]{2,1,0:T(8,128)(2,1)S(1)}, bf16[1,448,2048]{2,1,0:T(8,128)(2,1)}, u32[]{:S(2)}) copy-start(bf16[1,448,2048]{2,1,0:T(8,128)(2,1)} %param.10) | copy-start | bytes 5505028
  0.0 101.7 %copy-start.2 = (f32[448]{0:T(512)S(1)}, f32[448]{0:T(512)}, u32[]{:S(2)}) copy-start(f32[448]{0:T(512)} %param.7) | copy-start | bytes 5380
  6.1 95.1 %all-to-all-start = ((bf16[64,8,448]{2,1,0:T(8,128)(2,1)}), bf16[64,8,448]{2,1,0:T(8,128)(2,1)S(1)}, u32[]{:S(2)}, u32[]{:S(2)}) async-start(bf16[64,8,448]{2,1,0:T(8,128)(2,1)} %bitcast.1), calls=%async_computation | async-start | bytes 1048576 | tf_op jit(solution)/shard_map/all_to_all | solution.py:78
  137.6 17.8 %copy-start.1 = (bf16[1,1024,448]{1,2,0:T(8,128)(2,1)S(1)}, bf16[1,1024,448]{1,2,0:T(8,128)(2,1)}, u32[]{:S(2)}) copy-start(bf16[1,1024,448]{1,2,0:T(8,128)(2,1)} %param.11) | copy-start | bytes 2752516

commit v2 on v0

v2 whole, which is shorter than its diff:
```python
import functools

import jax
import jax.numpy as jnp
from jax import lax
from jax.experimental import pallas as pl
from jax.experimental.pallas import tpu as pltpu
from jax.sharding import PartitionSpec as P

D = 7168


NORM_EPS = 1e-06
LANES = 128
CORES = 2


def place_rows(experts, capacity, routes_ref, tokens_ref, rows_ref, target_ref):
    slots = rows_ref.shape[0]
    count = tokens_ref.shape[1]
    first, second = routes_ref[0:1, :], routes_ref[1:2, :]
    names = lax.broadcasted_iota(jnp.int32, (experts, count), 0)
    one = (names == first).astype(jnp.float32)
    two = (names == second).astype(jnp.float32)
    earlier = lax.broadcasted_iota(jnp.int32, (count, count), 0) < lax.broadcasted_iota(
        jnp.int32, (count, count), 1
    )
    before = jnp.dot(
        (one + two).astype(jnp.bfloat16),
        earlier.astype(jnp.float32).astype(jnp.bfloat16),
        preferred_element_type=jnp.float32,
    )
    place_one = jnp.sum(one * before, axis=0, keepdims=True).astype(jnp.int32)
    place_two = jnp.sum(two * (before + one), axis=0, keepdims=True).astype(jnp.int32)
    slot_one, slot_two = first * capacity + place_one, second * capacity + place_two
    target_ref[0:1, :] = slot_one
    target_ref[1:2, :] = slot_two
    row = lax.broadcasted_iota(jnp.int32, (slots, count), 0)
    picked = jnp.where((row == slot_one) | (row == slot_two), 1.0, 0.0).astype(jnp.bfloat16)
    rows_ref[...] = lax.dot_general(
        picked, tokens_ref[...], (((1,), (1,)), ((), ())), preferred_element_type=jnp.float32
    ).astype(jnp.bfloat16)


def split_rows(values):
    high = lax.reduce_precision(values, 8, 7)
    low = values - high
    column = jnp.arange(LANES, dtype=jnp.int32)[None, :]
    block = jnp.where(column == 0, high[:, None], jnp.where(column == 1, low[:, None], 0.0))
    return block.astype(jnp.bfloat16)


def partial_rows(arrived, norm_gain, w_gate_up):
    values = arrived.astype(jnp.float32)
    squares = jnp.sum(values * values, axis=1)
    gained = (values * norm_gain[None, :]).astype(jnp.bfloat16)
    partial = jnp.dot(gained, w_gate_up, preferred_element_type=jnp.float32).astype(jnp.bfloat16)
    return jnp.concatenate([partial, split_rows(squares)], axis=1)


def exchange(values, axis, members):
    return lax.all_to_all(
        values, axis, split_axis=0, concat_axis=0, tiled=True, axis_index_groups=members
    )


def local(tokens, norm_gain, route_expert, route_gate, w_gate_up, w_down):
    tok_rows, width = tokens.shape
    groups = lax.axis_size("group")
    ways = lax.axis_size("slot")
    chips = groups // CORES
    picks = route_expert.shape[1]
    capacity = 2 * tok_rows * picks // groups
    slots = groups * capacity
    half = chips * capacity
    both = w_gate_up.shape[2]
    inner = both // 2
    columns = [[CORES * chip + core for chip in range(chips)] for core in range(CORES)]
    swap = [(index, index ^ 1) for index in range(groups)]
    every = [list(range(ways))]

    routes = route_expert.T ^ (lax.axis_index("group") % CORES)
    rows, target = pl.pallas_call(
        functools.partial(place_rows, groups, capacity),
        out_shape=(
            jax.ShapeDtypeStruct((slots, width), jnp.bfloat16),
            jax.ShapeDtypeStruct((picks, tok_rows), jnp.int32),
        ),
        name="place_rows",
    )(routes, tokens.T)
    gates = route_gate.T
    row = lax.broadcasted_iota(jnp.int32, (slots, tok_rows), 0)
    weights_back = jnp.where(row == target[0:1], gates[0:1], 0) + jnp.where(
        row == target[1:2], gates[1:2], 0
    )

    arrived = exchange(rows.reshape(chips, CORES * capacity, width), "group", columns)
    other_gate_up = lax.ppermute(w_gate_up, "group", swap)
    other_down = lax.ppermute(w_down, "group", swap)
    arrived = arrived.reshape(chips, CORES, capacity, width)
    sent = jnp.concatenate(
        [
            partial_rows(arrived[:, 0].reshape(half, width), norm_gain, w_gate_up[0]),
            partial_rows(arrived[:, 1].reshape(half, width), norm_gain, other_gate_up[0]),
        ],
        axis=0,
    )
    pieces = exchange(sent.reshape(ways, slots // ways, both + LANES), "slot", every)
    mine = jnp.sum(pieces.astype(jnp.float32), axis=0)
    scale = lax.rsqrt((mine[:, both : both + 1] + mine[:, both + 1 : both + 2]) / D + NORM_EPS)
    gate, up = mine[:, :inner] * scale, mine[:, inner:both] * scale
    hidden = (jax.nn.silu(gate) * up).astype(jnp.bfloat16)
    spread = exchange(jnp.broadcast_to(hidden[None], (ways,) + hidden.shape), "slot", every)
    spread = spread.reshape(slots, inner)
    finished = jnp.concatenate(
        [
            jnp.dot(spread[:half], w_down[0], preferred_element_type=jnp.float32)
            .astype(jnp.bfloat16)
            .reshape(chips, capacity, width),
            jnp.dot(spread[half:], other_down[0], preferred_element_type=jnp.float32)
            .astype(jnp.bfloat16)
            .reshape(chips, capacity, width),
        ],
        axis=1,
    )
    returned = exchange(finished, "group", columns).reshape(slots, width)
    mixed = lax.dot_general(
        returned, weights_back, (((0,), (0,)), ((), ())), preferred_element_type=jnp.float32
    )
    return mixed.astype(jnp.bfloat16).T


def solution(mesh):
    placed = (
        P("group", "slot"),
        P("slot"),
        P("group", None),
        P("group", None),
        P("group", "slot", None),
        P("group", None, "slot"),
    )
    return jax.shard_map(
        local, mesh=mesh, in_specs=placed, out_specs=P("group", "slot"), check_vma=False
    )
```

time: 420 us -> 228 us (0.54)
  blocking collectives: 217 us -> 34.1 us
  starting transfers between devices: 0.04 us -> 42.8 us
  waiting for transfers between devices: 175 us -> 138 us
  between operations: 13.5 us -> 0.21 us
    all_to_all x2 -> x1, blocking collectives: 172 us -> 34.1 us  [exchange(): lax.all_to_all(values, axis, split_axis=0, concat_axis=0, tiled=True, axi...]
    all_to_all x0 -> x3, waiting for transfers between devices: none -> 138 us  [exchange(): lax.all_to_all(values, axis, split_axis=0, concat_axis=0, tiled=True, axi...]
    reduce_scatter x1 -> x0, waiting for transfers between devices: 94.1 us -> none  [expert_rows(): lax.psum_scatter(jnp.dot(arrived, w_gate_up[0], preferred_element_type=jn...]
    all_gather x1 -> x0, waiting for transfers between devices: 81.1 us -> none  [expert_rows(): lax.all_gather(hidden, 'slot', axis=0, tiled=True)]
    psum x1 -> x0, blocking collectives: 44.6 us -> none  [local(): squares = lax.psum(jnp.sum(values * values, axis=1), 'slot')]
    all_to_all x0 -> x3, starting transfers between devices: none -> 39 us  [exchange(): lax.all_to_all(values, axis, split_axis=0, concat_axis=0, tiled=True, axi...]
  transfers between devices with their start and end apart: 2 -> 5, of which waited for: 2 -> 3; matrix products, arithmetic and copies ran while one was open for 0% -> 1% of each run, Pallas kernels for 0% -> 0%
where the time goes in v2:
time: 228 us; the launch traced here: 227 us
  waiting for transfers between devices  138 us (61%)
  starting transfers between devices  42.8 us (19%)
  blocking collectives  34.1 us (15%)
  matrix products  4.81 us (2%)
  other arithmetic  3.34 us (1%)
    all_to_all x3, waiting for transfers between devices, exchange(): lax.all_to_all(values, axis, split_axis=0, concat_axis=0, tiled=True, axi...  138 us
    all_to_all x3, starting transfers between devices, exchange(): lax.all_to_all(values, axis, split_axis=0, concat_axis=0, tiled=True, axi...  39 us
    all_to_all x1, blocking collectives, exchange(): lax.all_to_all(values, axis, split_axis=0, concat_axis=0, tiled=True, axi...  34.1 us
  transfers between devices with their start and end apart: 5, of which 3 were waited for; matrix products, arithmetic and copies ran while one was open for 1% of the time, Pallas kernels for 0%

profile of v2, /device:TPU:6, one launch (start us, length us, event | category | flops | bytes accessed | tf_op | source)
XLA Modules:
  0.0 227.0 jit_solution(13157452542409545265)
XLA Ops:
  0.0 1.2 xor_bitcast_fusion.routes_ref
  1.2 2.1 place_rows.1
  3.4 28.9 %all-to-all-start = ((bf16[32,16,448]{2,1,0:T(8,128)(2,1)}), bf16[32,16,448]{2,1,0:T(8,128)(2,1)S(1)}, u32[]{:S(2)}, u32[]{:S(2)}) async-start(bf16[32,16,448]{2,1,0:T(8,128)(2,1)} %bitcast.50), calls=%async_computation | async-start | bytes 1048576 | tf_op jit(solution)/shard_map/all_to_all | solution.py:62
  32.3 1.9 collective-permute-start
  34.2 62.9 %all-to-all-done = bf16[32,16,448]{2,1,0:T(8,128)(2,1)S(1)} async-done(((bf16[32,16,448]{2,1,0:T(8,128)(2,1)}), bf16[32,16,448]{2,1,0:T(8,128)(2,1)S(1)}, u32[]{:S(2)}, u32[]{:S(2)}) %all-to-all-start) | async-done | bytes 458784 | tf_op jit(solution)/shard_map/all_to_all | solution.py:62
  97.1 0.2 fusion.5
  97.5 0.2 select_convert_fusion.1
  97.7 2.2 convolution_convert_fusion.1
  100.0 0.7 convolution_convert_fusion
  100.7 0.2 maximum_maximum_fusion
  100.9 34.1 %all_to_all.20 = bf16[16,32,2176]{2,1,0:T(8,128)(2,1)S(1)} all-to-all(bf16[16,32,2176]{2,1,0:T(8,128)(2,1)S(1)} %bitcast.41), channel_id=1, replica_groups={{0,1,2,3,4,5,6,7,8,9,10,11,12,13,14,15},{16,17,18,19,20,21,22,23,24,25,..., dimensions={0} | all-to-all | bytes 4456448 | tf_op jit(solution)/shard_map/all_to_all | solution.py:62
  135.0 0.3 convert_reduce_fusion
  135.3 0.2 fusion.31
  135.7 1.1 broadcast_in_dim.105
  136.7 5.8 %all-to-all-start.2 = ((bf16[16,32,1024]{2,1,0:T(8,128)(2,1)}), bf16[16,32,1024]{2,1,0:T(8,128)(2,1)S(1)}, u32[]{:S(2)}, u32[]{:S(2)}) async-start(bf16[16,32,1024]{2,1,0:T(8,128)(2,1)} %broadcast_in_dim.105), calls=%async_computation.2 | async-start | bytes 2097152 | tf_op jit(solution)/shard_map/all_to_all | solution.py:62
  142.5 1.9 collective-permute-start.1
  144.4 10.9 %all-to-all-done.2 = bf16[16,32,1024]{2,1,0:T(8,128)(2,1)S(1)} async-done(((bf16[16,32,1024]{2,1,0:T(8,128)(2,1)}), bf16[16,32,1024]{2,1,0:T(8,128)(2,1)S(1)}, u32[]{:S(2)}, u32[]{:S(2)}) %all-to-all-start.2) | async-done | bytes 1048608 | tf_op jit(solution)/shard_map/all_to_all | solution.py:62
  155.5 0.4 convolution_convert_fusion.2
  155.9 0.1 copy.14
  156.1 0.4 convolution_convert_fusion.3
  156.7 0.9 pad_maximum_fusion
  157.5 4.3 %all-to-all-start.3 = ((bf16[32,16,448]{2,1,0:T(8,128)(2,1)}), bf16[32,16,448]{2,1,0:T(8,128)(2,1)S(1)}, u32[]{:S(2)}, u32[]{:S(2)}) async-start(bf16[32,16,448]{2,1,0:T(8,128)(2,1)} %pad_maximum_fusion), calls=%async_computation.3 | async-start | bytes 1048576 | tf_op jit(solution)/shard_map/all_to_all | solution.py:62
  161.9 64.1 %all-to-all-done.3 = bf16[32,16,448]{2,1,0:T(8,128)(2,1)S(1)} async-done(((bf16[32,16,448]{2,1,0:T(8,128)(2,1)}), bf16[32,16,448]{2,1,0:T(8,128)(2,1)S(1)}, u32[]{:S(2)}, u32[]{:S(2)}) %all-to-all-start.3) | async-done | bytes 458784 | tf_op jit(solution)/shard_map/all_to_all | solution.py:62
  226.0 1.0 convolution_convert_fusion.4
  (19 shorter events, 0.6 us)
Async XLA Ops:
  3.4 96.6 %copy-start.1 = (f32[448]{0:T(512)S(1)}, f32[448]{0:T(512)}, u32[]{:S(2)}) copy-start(f32[448]{0:T(512)} %param.7) | copy-start | bytes 5380
  3.4 93.7 %all-to-all-start = ((bf16[32,16,448]{2,1,0:T(8,128)(2,1)}), bf16[32,16,448]{2,1,0:T(8,128)(2,1)S(1)}, u32[]{:S(2)}, u32[]{:S(2)}) async-start(bf16[32,16,448]{2,1,0:T(8,128)(2,1)} %bitcast.50), calls=%async_computation | async-start | bytes 1048576 | tf_op jit(solution)/shard_map/all_to_all | solution.py:62
  32.3 67.7 %collective-permute-start = (bf16[1,448,2048]{2,1,0:T(8,128)(2,1)}, bf16[1,448,2048]{2,1,0:T(8,128)(2,1)S(1)}, u32[]{:S(2)}, u32[]{:S(2)}) collective-permute-start(bf16[1,448,2048]{2,1,0:T(8,128)(2,1)} %param.10), channel_id=1, source_target_pairs={{0,16},{16,0},{32,48},{48,32},{64,80},{80,64},{96,112},{112,96},{1... | collective-permute-start | bytes 5505032 | tf_op jit(solution)/shard_map/ppermute | solution.py:98
  135.3 7.2 %copy-start = (bf16[1,1024,448]{1,2,0:T(8,128)(2,1)S(1)}, bf16[1,1024,448]{1,2,0:T(8,128)(2,1)}, u32[]{:S(2)}) copy-start(bf16[1,1024,448]{1,2,0:T(8,128)(2,1)} %param.11) | copy-start | bytes 2752516
  136.7 18.6 %all-to-all-start.2 = ((bf16[16,32,1024]{2,1,0:T(8,128)(2,1)}), bf16[16,32,1024]{2,1,0:T(8,128)(2,1)S(1)}, u32[]{:S(2)}, u32[]{:S(2)}) async-start(bf16[16,32,1024]{2,1,0:T(8,128)(2,1)} %broadcast_in_dim.105), calls=%async_computation.2 | async-start | bytes 2097152 | tf_op jit(solution)/shard_map/all_to_all | solution.py:62
  142.5 12.9 %collective-permute-start.1 = (bf16[1,1024,448]{1,2,0:T(8,128)(2,1)S(1)}, bf16[1,1024,448]{1,2,0:T(8,128)(2,1)S(1)}, u32[]{:S(2)}, u32[]{:S(2)}) collective-permute-start(bf16[1,1024,448]{1,2,0:T(8,128)(2,1)S(1)} %copy-done), channel_id=1, source_target_pairs={{0,16},{16,0},{32,48},{48,32},{64,80},{80,64},{96,112},{112,96},{1... | collective-permute-start | bytes 2752520 | tf_op jit(solution)/shard_map/ppermute | solution.py:99
  156.1 5.8 %copy-start.2 = (bf16[128,2]{0,1:T(2,128)(2,1)S(1)}, bf16[128,2]{0,1:T(2,128)(2,1)}, u32[]{:S(2)}) copy-start(bf16[128,2]{0,1:T(2,128)(2,1)} %param.9) | copy-start | bytes 1540
  156.1 5.9 %copy-start.3 = (s32[2,128]{1,0:T(2,128)S(1)}, s32[2,128]{1,0:T(2,128)}, u32[]{:S(2)}) copy-start(s32[2,128]{1,0:T(2,128)} %get-tuple-element.7) | copy-start | bytes 3076
  157.5 68.5 %all-to-all-start.3 = ((bf16[32,16,448]{2,1,0:T(8,128)(2,1)}), bf16[32,16,448]{2,1,0:T(8,128)(2,1)S(1)}, u32[]{:S(2)}, u32[]{:S(2)}) async-start(bf16[32,16,448]{2,1,0:T(8,128)(2,1)} %pad_maximum_fusion), calls=%async_computation.3 | async-start | bytes 1048576 | tf_op jit(solution)/shard_map/all_to_all | solution.py:62

commit v3 on v2

--- a/solution.py
+++ b/solution.py
@@ -12,13 +12,16 @@
 
 NORM_EPS = 1e-06
 LANES = 128
+STRIP = 512
+VMEM_BYTES = 32 * 1024 * 1024
 CORES = 2
 
 
 def place_rows(experts, capacity, routes_ref, tokens_ref, rows_ref, target_ref):
     slots = rows_ref.shape[0]
     count = tokens_ref.shape[1]
-    first, second = routes_ref[0:1, :], routes_ref[1:2, :]
+    core = lax.rem(lax.axis_index("group"), CORES)
+    first, second = routes_ref[0:1, :] ^ core, routes_ref[1:2, :] ^ core
     names = lax.broadcasted_iota(jnp.int32, (experts, count), 0)
     one = (names == first).astype(jnp.float32)
     two = (names == second).astype(jnp.float32)
@@ -42,20 +45,40 @@
     ).astype(jnp.bfloat16)
 
 
-def split_rows(values):
-    high = lax.reduce_precision(values, 8, 7)
-    low = values - high
-    column = jnp.arange(LANES, dtype=jnp.int32)[None, :]
-    block = jnp.where(column == 0, high[:, None], jnp.where(column == 1, low[:, None], 0.0))
-    return block.astype(jnp.bfloat16)
+def partial_rows(arrived_ref, gain_ref, near_ref, far_ref, sent_ref):
+    half = sent_ref.shape[0] // CORES
+    both = far_ref.shape[1]
+    values = arrived_ref[...].astype(jnp.float32)
+    capacity = values.shape[1] // CORES
+    column = lax.broadcasted_iota(jnp.int32, (half, LANES), 1)
+    for which, weights in enumerate((near_ref, far_ref)):
+        mine = values[:, which * capacity : (which + 1) * capacity].reshape(half, -1)
+        squares = jnp.sum(mine * mine, axis=1, keepdims=True)
+        high = squares.astype(jnp.bfloat16).astype(jnp.float32)
+        gained = (mine * gain_ref[0:1, :]).astype(jnp.bfloat16)
+        rows = slice(which * half, (which + 1) * half)
+        sent_ref[rows, both:] = jnp.where(
+            column == 0, high, jnp.where(column == 1, squares - high, 0.0)
+        ).astype(jnp.bfloat16)
+        for start in range(0, both, STRIP):
+            sent_ref[rows, start : start + STRIP] = jnp.dot(
+                gained, weights[:, start : start + STRIP], preferred_element_type=jnp.float32
+            ).astype(jnp.bfloat16)
 
 
-def partial_rows(arrived, norm_gain, w_gate_up):
-    values = arrived.astype(jnp.float32)
-    squares = jnp.sum(values * values, axis=1)
-    gained = (values * norm_gain[None, :]).astype(jnp.bfloat16)
-    partial = jnp.dot(gained, w_gate_up, preferred_element_type=jnp.float32).astype(jnp.bfloat16)
-    return jnp.concatenate([partial, split_rows(squares)], axis=1)
+def down_rows(hidden_ref, near_ref, far_ref, finished_ref):
+    half = hidden_ref.shape[0] // CORES
+    chips, capacity, width = finished_ref.shape
+    results = [
+        lax.dot_general(
+            hidden_ref[which * half : (which + 1) * half, :],
+            weights[...],
+            (((1,), (1,)), ((), ())),
+            preferred_element_type=jnp.float32,
+        ).reshape(chips, capacity // CORES, width)
+        for which, weights in enumerate((near_ref, far_ref))
+    ]
+    finished_ref[...] = jnp.concatenate(results, axis=1).astype(jnp.bfloat16)
 
 
 def exchange(values, axis, members):
@@ -72,14 +95,12 @@
     picks = route_expert.shape[1]
     capacity = 2 * tok_rows * picks // groups
     slots = groups * capacity
-    half = chips * capacity
     both = w_gate_up.shape[2]
     inner = both // 2
     columns = [[CORES * chip + core for chip in range(chips)] for core in range(CORES)]
     swap = [(index, index ^ 1) for index in range(groups)]
     every = [list(range(ways))]
 
-    routes = route_expert.T ^ (lax.axis_index("group") % CORES)
     rows, target = pl.pallas_call(
         functools.partial(place_rows, groups, capacity),
         out_shape=(
@@ -87,7 +108,7 @@
             jax.ShapeDtypeStruct((picks, tok_rows), jnp.int32),
         ),
         name="place_rows",
-    )(routes, tokens.T)
+    )(route_expert.T, tokens.T)
     gates = route_gate.T
     row = lax.broadcasted_iota(jnp.int32, (slots, tok_rows), 0)
     weights_back = jnp.where(row == target[0:1], gates[0:1], 0) + jnp.where(
@@ -97,32 +118,39 @@
     arrived = exchange(rows.reshape(chips, CORES * capacity, width), "group", columns)
     other_gate_up = lax.ppermute(w_gate_up, "group", swap)
     other_down = lax.ppermute(w_down, "group", swap)
-    arrived = arrived.reshape(chips, CORES, capacity, width)
-    sent = jnp.concatenate(
-        [
-            partial_rows(arrived[:, 0].reshape(half, width), norm_gain, w_gate_up[0]),
-            partial_rows(arrived[:, 1].reshape(half, width), norm_gain, other_gate_up[0]),
-        ],
-        axis=0,
+    whole = pl.BlockSpec(memory_space=pltpu.VMEM)
+    gain = jnp.broadcast_to(norm_gain[None], (8, width))
+    arrived, gain, other_gate_up, other_down, weights_back = lax.optimization_barrier(
+        (arrived, gain, other_gate_up, other_down, weights_back)
     )
+    sent = pl.pallas_call(
+        partial_rows,
+        out_shape=jax.ShapeDtypeStruct((slots, both + LANES), jnp.bfloat16),
+        in_specs=[whole] * 4,
+        out_specs=whole,
+        compiler_params=pltpu.CompilerParams(vmem_limit_bytes=VMEM_BYTES),
+        cost_estimate=pl.CostEstimate(
+            flops=2 * slots * width * both, bytes_accessed=8 * width * both, transcendentals=0
+        ),
+        name="partial_rows",
+    )(arrived, gain, w_gate_up[0], other_gate_up[0])
     pieces = exchange(sent.reshape(ways, slots // ways, both + LANES), "slot", every)
     mine = jnp.sum(pieces.astype(jnp.float32), axis=0)
     scale = lax.rsqrt((mine[:, both : both + 1] + mine[:, both + 1 : both + 2]) / D + NORM_EPS)
     gate, up = mine[:, :inner] * scale, mine[:, inner:both] * scale
     hidden = (jax.nn.silu(gate) * up).astype(jnp.bfloat16)
     spread = exchange(jnp.broadcast_to(hidden[None], (ways,) + hidden.shape), "slot", every)
-    spread = spread.reshape(slots, inner)
-    finished = jnp.concatenate(
-        [
-            jnp.dot(spread[:half], w_down[0], preferred_element_type=jnp.float32)
-            .astype(jnp.bfloat16)
-            .reshape(chips, capacity, width),
-            jnp.dot(spread[half:], other_down[0], preferred_element_type=jnp.float32)
-            .astype(jnp.bfloat16)
-            .reshape(chips, capacity, width),
-        ],
-        axis=1,
-    )
+    finished = pl.pallas_call(
+        down_rows,
+        out_shape=jax.ShapeDtypeStruct((chips, CORES * capacity, width), jnp.bfloat16),
+        in_specs=[whole] * 3,
+        out_specs=whole,
+        compiler_params=pltpu.CompilerParams(vmem_limit_bytes=VMEM_BYTES),
+        cost_estimate=pl.CostEstimate(
+            flops=2 * slots * width * inner, bytes_accessed=6 * width * inner, transcendentals=0
+        ),
+        name="down_rows",
+    )(spread.reshape(slots, inner), w_down[0].T, other_down[0].T)
     returned = exchange(finished, "group", columns).reshape(slots, width)
     mixed = lax.dot_general(
         returned, weights_back, (((0,), (0,)), ((), ())), preferred_element_type=jnp.float32

time: 228 us -> 223 us (0.978)
  blocking collectives: 34.1 us -> 121 us
  waiting for transfers between devices: 138 us -> 58.9 us
  starting transfers between devices: 42.8 us -> 33.1 us
  matrix products: 4.81 us -> 1 us
  other arithmetic: 3.34 us -> 0.69 us
    all_to_all x1 -> x3, blocking collectives: 34.1 us -> 121 us  [exchange(): lax.all_to_all(values, axis, split_axis=0, concat_axis=0, tiled=True, axi...]
    all_to_all x3 -> x1, waiting for transfers between devices: 138 us -> 57.6 us  [exchange(): lax.all_to_all(values, axis, split_axis=0, concat_axis=0, tiled=True, axi...]
    all_to_all x3 -> x1, starting transfers between devices: 39 us -> 28.7 us  [exchange(): lax.all_to_all(values, axis, split_axis=0, concat_axis=0, tiled=True, axi...]
    dot_general x4 -> x0, matrix products: 3.82 us -> none  [the longest x2 2.94 us: partial_rows(): jnp.dot(gained, w_gate_up, preferred_element_type=jnp.float32)]
  transfers between devices with their start and end apart: 5 -> 3, of which waited for: 3 -> 2; matrix products, arithmetic and copies ran while one was open for 1% -> 1% of each run, Pallas kernels for 0% -> 0%
where the time goes in v3:
time: 223 us; the launch traced here: 222 us
  blocking collectives  121 us (54%)
  waiting for transfers between devices  58.9 us (26%)
  starting transfers between devices  33.1 us (15%)
  Pallas kernels  4.11 us (2%)
  local copies, waits for them, and re-layouts  3.8 us (2%)
    all_to_all x3, blocking collectives, exchange(): lax.all_to_all(values, axis, split_axis=0, concat_axis=0, tiled=True, axi...  121 us
    all_to_all x1, waiting for transfers between devices, exchange(): lax.all_to_all(values, axis, split_axis=0, concat_axis=0, tiled=True, axi...  57.6 us
    all_to_all x1, starting transfers between devices, exchange(): lax.all_to_all(values, axis, split_axis=0, concat_axis=0, tiled=True, axi...  28.7 us
  transfers between devices with their start and end apart: 3, of which 2 were waited for; matrix products, arithmetic and copies ran while one was open for 1% of the time, Pallas kernels for 0%

profile of v3, /device:TPU:6, one launch (start us, length us, event | category | flops | bytes accessed | tf_op | source)
XLA Modules:
  0.0 222.2 jit_solution(788350394607622054)
XLA Ops:
  0.0 2.1 place_rows.1
  2.1 28.7 %all-to-all-start = ((bf16[32,16,448]{2,1,0:T(8,128)(2,1)}), bf16[32,16,448]{2,1,0:T(8,128)(2,1)S(1)}, u32[]{:S(2)}, u32[]{:S(2)}) async-start(bf16[32,16,448]{2,1,0:T(8,128)(2,1)} %bitcast.32), calls=%async_computation | async-start | bytes 1048576 | tf_op jit(solution)/shard_map/all_to_all | solution.py:85
  30.9 1.9 collective-permute-start
  32.8 2.4 %collective-permute-start.1 = (bf16[1,1024,448]{1,2,0:T(8,128)(2,1)}, bf16[1,1024,448]{1,2,0:T(8,128)(2,1)S(1)}, u32[]{:S(2)}, u32[]{:S(2)}) collective-permute-start(bf16[1,1024,448]{1,2,0:T(8,128)(2,1)} %param.11), channel_id=1, source_target_pairs={{0,16},{16,0},{32,48},{48,32},{64,80},{80,64},{96,112},{112,96},{1... | collective-permute-start | bytes 2752520 | tf_op jit(solution)/shard_map/ppermute | solution.py:120
  35.2 0.7 slice_bitcast_fusion.2
  36.0 0.8 slice_bitcast_fusion.3
  36.7 0.1 fusion.2
  36.8 1.3 collective-permute-done.1
  38.1 0.0 collective-permute-done
  38.1 57.6 %all-to-all-done.arrived_ref = bf16[32,16,448]{2,1,0:T(8,128)(2,1)S(1)} async-done(((bf16[32,16,448]{2,1,0:T(8,128)(2,1)}), bf16[32,16,448]{2,1,0:T(8,128)(2,1)S(1)}, u32[]{:S(2)}, u32[]{:S(2)}) %all-to-all-start) | async-done | bytes 458784 | tf_op jit(solution)/shard_map/all_to_all | solution.py:85
  95.7 0.7 broadcast_in_dim.34.gain_ref
  96.4 1.5 copy-done
  97.9 1.3 partial_rows.1
  99.2 34.1 %all_to_all.20 = bf16[16,32,2176]{2,1,0:T(8,128)(2,1)S(1)} all-to-all(bf16[16,32,2176]{2,1,0:T(8,128)(2,1)S(1)} %bitcast.25), channel_id=1, replica_groups={{0,1,2,3,4,5,6,7,8,9,10,11,12,13,14,15},{16,17,18,19,20,21,22,23,24,25,..., dimensions={0} | all-to-all | bytes 4456448 | tf_op jit(solution)/shard_map/all_to_all | solution.py:85
  133.3 0.3 convert_reduce_fusion
  133.6 0.0 copy-start.1
  133.6 0.2 fusion.8
  133.8 0.1 fusion.4
  134.0 0.1 broadcast_in_dim.40
  134.1 17.6 %all_to_all.21 = bf16[16,32,1024]{2,1,0:T(8,128)(2,1)S(1)} all-to-all(bf16[16,32,1024]{2,1,0:T(8,128)(2,1)S(1)} %broadcast_in_dim.40), channel_id=1, replica_groups={{0,1,2,3,4,5,6,7,8,9,10,11,12,13,14,15},{16,17,18,19,20,21,22,23,24,25,..., dimensions={0} | all-to-all | bytes 2097152 | tf_op jit(solution)/shard_map/all_to_all | solution.py:85
  151.7 0.0 copy-done.1
  151.7 0.7 down_rows.1
  152.4 68.7 %all_to_all.22 = bf16[32,16,448]{2,1,0:T(8,128)(2,1)S(1)} all-to-all(bf16[32,16,448]{2,1,0:T(8,128)(2,1)S(1)} %down_rows.1), channel_id=1, replica_groups={{0,32,64,96,128,160,192,224,256,288,320,352,384,416,448,480,512,544,576..., dimensions={0} | all-to-all | bytes 917504 | tf_op jit(solution)/shard_map/all_to_all | solution.py:85
  221.2 1.0 convolution_convert_fusion
  (1 shorter events, 0.0 us)
Async XLA Ops:
  2.1 93.6 %all-to-all-start = ((bf16[32,16,448]{2,1,0:T(8,128)(2,1)}), bf16[32,16,448]{2,1,0:T(8,128)(2,1)S(1)}, u32[]{:S(2)}, u32[]{:S(2)}) async-start(bf16[32,16,448]{2,1,0:T(8,128)(2,1)} %bitcast.32), calls=%async_computation | async-start | bytes 1048576 | tf_op jit(solution)/shard_map/all_to_all | solution.py:85
  30.9 7.2 %collective-permute-start = (bf16[1,448,2048]{2,1,0:T(8,128)(2,1)}, bf16[1,448,2048]{2,1,0:T(8,128)(2,1)S(1)}, u32[]{:S(2)}, u32[]{:S(2)}) collective-permute-start(bf16[1,448,2048]{2,1,0:T(8,128)(2,1)} %param.10), channel_id=1, source_target_pairs={{0,16},{16,0},{32,48},{48,32},{64,80},{80,64},{96,112},{112,96},{1... | collective-permute-start | bytes 5505032 | tf_op jit(solution)/shard_map/ppermute | solution.py:119
  32.8 5.3 %collective-permute-start.1 = (bf16[1,1024,448]{1,2,0:T(8,128)(2,1)}, bf16[1,1024,448]{1,2,0:T(8,128)(2,1)S(1)}, u32[]{:S(2)}, u32[]{:S(2)}) collective-permute-start(bf16[1,1024,448]{1,2,0:T(8,128)(2,1)} %param.11), channel_id=1, source_target_pairs={{0,16},{16,0},{32,48},{48,32},{64,80},{80,64},{96,112},{112,96},{1... | collective-permute-start | bytes 2752520 | tf_op jit(solution)/shard_map/ppermute | solution.py:120
  96.4 1.5 copy-start
  133.6 18.1 %copy-start.1 = (bf16[1,1024,448]{1,2,0:T(8,128)(2,1)S(1)}, bf16[1,1024,448]{1,2,0:T(8,128)(2,1)}, u32[]{:S(2)}) copy-start(bf16[1,1024,448]{1,2,0:T(8,128)(2,1)} %param.11) | copy-start | bytes 2752516

commit v4 on v3

--- a/solution.py
+++ b/solution.py
@@ -45,25 +45,27 @@
     ).astype(jnp.bfloat16)
 
 
-def partial_rows(arrived_ref, gain_ref, near_ref, far_ref, sent_ref):
-    half = sent_ref.shape[0] // CORES
-    both = far_ref.shape[1]
+def partial_rows(which, arrived_ref, *refs):
+    weights, sent_ref = refs[:-1], refs[-1]
+    half, columns = sent_ref.shape
+    both = columns - LANES
     values = arrived_ref[...].astype(jnp.float32)
     capacity = values.shape[1] // CORES
     column = lax.broadcasted_iota(jnp.int32, (half, LANES), 1)
-    for which, weights in enumerate((near_ref, far_ref)):
-        mine = values[:, which * capacity : (which + 1) * capacity].reshape(half, -1)
-        squares = jnp.sum(mine * mine, axis=1, keepdims=True)
-        high = squares.astype(jnp.bfloat16).astype(jnp.float32)
-        gained = (mine * gain_ref[0:1, :]).astype(jnp.bfloat16)
-        rows = slice(which * half, (which + 1) * half)
-        sent_ref[rows, both:] = jnp.where(
-            column == 0, high, jnp.where(column == 1, squares - high, 0.0)
-        ).astype(jnp.bfloat16)
-        for start in range(0, both, STRIP):
-            sent_ref[rows, start : start + STRIP] = jnp.dot(
-                gained, weights[:, start : start + STRIP], preferred_element_type=jnp.float32
+    mine = values[:, which * capacity : (which + 1) * capacity].reshape(half, -1)
+    exact = mine.astype(jnp.bfloat16)
+    squares = jnp.sum(mine * mine, axis=1, keepdims=True)
+    high = squares.astype(jnp.bfloat16).astype(jnp.float32)
+    sent_ref[:, both:] = jnp.where(
+        column == 0, high, jnp.where(column == 1, squares - high, 0.0)
+    ).astype(jnp.bfloat16)
+    done = 0
+    for part in weights:
+        for start in range(0, part.shape[1], STRIP):
+            sent_ref[:, done : done + STRIP] = jnp.dot(
+                exact, part[:, start : start + STRIP], preferred_element_type=jnp.float32
             ).astype(jnp.bfloat16)
+            done += STRIP
 
 
 def down_rows(hidden_ref, near_ref, far_ref, finished_ref):
@@ -116,24 +118,31 @@
     )
 
     arrived = exchange(rows.reshape(chips, CORES * capacity, width), "group", columns)
-    other_gate_up = lax.ppermute(w_gate_up, "group", swap)
+    gained = (w_gate_up[0].astype(jnp.float32) * norm_gain[:, None]).astype(jnp.bfloat16)
+    other_gate = lax.ppermute(gained[:, :inner], "group", swap)
+    other_up = lax.ppermute(gained[:, inner:], "group", swap)
     other_down = lax.ppermute(w_down, "group", swap)
     whole = pl.BlockSpec(memory_space=pltpu.VMEM)
-    gain = jnp.broadcast_to(norm_gain[None], (8, width))
-    arrived, gain, other_gate_up, other_down, weights_back = lax.optimization_barrier(
-        (arrived, gain, other_gate_up, other_down, weights_back)
+    arrived, gained, other_gate, other_up, other_down, weights_back = lax.optimization_barrier(
+        (arrived, gained, other_gate, other_up, other_down, weights_back)
     )
-    sent = pl.pallas_call(
-        partial_rows,
-        out_shape=jax.ShapeDtypeStruct((slots, both + LANES), jnp.bfloat16),
-        in_specs=[whole] * 4,
-        out_specs=whole,
-        compiler_params=pltpu.CompilerParams(vmem_limit_bytes=VMEM_BYTES),
-        cost_estimate=pl.CostEstimate(
-            flops=2 * slots * width * both, bytes_accessed=8 * width * both, transcendentals=0
-        ),
-        name="partial_rows",
-    )(arrived, gain, w_gate_up[0], other_gate_up[0])
+
+    def products(which, *weights):
+        return pl.pallas_call(
+            functools.partial(partial_rows, which),
+            out_shape=jax.ShapeDtypeStruct((slots // CORES, both + LANES), jnp.bfloat16),
+            in_specs=[whole] * (1 + len(weights)),
+            out_specs=whole,
+            compiler_params=pltpu.CompilerParams(vmem_limit_bytes=VMEM_BYTES),
+            cost_estimate=pl.CostEstimate(
+                flops=slots * width * both, bytes_accessed=4 * width * both, transcendentals=0
+            ),
+            name="partial_rows",
+        )(arrived, *weights)
+
+    sent = jnp.concatenate(
+        [products(0, gained), products(1, other_gate, other_up)], axis=0
+    )
     pieces = exchange(sent.reshape(ways, slots // ways, both + LANES), "slot", every)
     mine = jnp.sum(pieces.astype(jnp.float32), axis=0)
     scale = lax.rsqrt((mine[:, both : both + 1] + mine[:, both + 1 : both + 2]) / D + NORM_EPS)

time: 223 us -> 222 us (level)
  waiting for transfers between devices: 58.9 us -> 54.5 us
    all_to_all x1, waiting for transfers between devices: 57.6 us -> 53.1 us  [exchange(): lax.all_to_all(values, axis, split_axis=0, concat_axis=0, tiled=True, axi...]
    ppermute x1 -> x2, starting transfers between devices: 1.92 us -> 4.33 us  [the longest x1 2.41 us: local(): other_up = lax.ppermute(gained[:, inner:], 'group', swap)]
  transfers between devices with their start and end apart: 3 -> 4, of which waited for: 2 -> 2; matrix products, arithmetic and copies ran while one was open for 1% -> 1% of each run, Pallas kernels for 0% -> 0%
where the time goes in v4:
time: 222 us; the launch traced here: 221 us
  blocking collectives  121 us (55%)
  waiting for transfers between devices  54.5 us (25%)
  starting transfers between devices  35 us (16%)
  Pallas kernels  4.27 us (2%)
  local copies, waits for them, and re-layouts  2.96 us (1%)
  other arithmetic  2.72 us (1%)
    all_to_all x3, blocking collectives, exchange(): lax.all_to_all(values, axis, split_axis=0, concat_axis=0, tiled=True, axi...  121 us
    all_to_all x1, waiting for transfers between devices, exchange(): lax.all_to_all(values, axis, split_axis=0, concat_axis=0, tiled=True, axi...  53.1 us
    all_to_all x1, starting transfers between devices, exchange(): lax.all_to_all(values, axis, split_axis=0, concat_axis=0, tiled=True, axi...  28.7 us
  transfers between devices with their start and end apart: 4, of which 2 were waited for; matrix products, arithmetic and copies ran while one was open for 1% of the time, Pallas kernels for 0%

profile of v4, /device:TPU:6, one launch (start us, length us, event | category | flops | bytes accessed | tf_op | source)
XLA Modules:
  0.0 221.1 jit_solution(1700809546075311616)
XLA Ops:
  0.0 2.1 place_rows.1
  2.1 28.7 %all-to-all-start = ((bf16[32,16,448]{2,1,0:T(8,128)(2,1)}), bf16[32,16,448]{2,1,0:T(8,128)(2,1)S(1)}, u32[]{:S(2)}, u32[]{:S(2)}) async-start(bf16[32,16,448]{2,1,0:T(8,128)(2,1)} %bitcast.31), calls=%async_computation | async-start | bytes 1048576 | tf_op jit(solution)/shard_map/all_to_all | solution.py:87
  30.9 1.9 collective-permute-start.2
  32.8 1.9 fusion.refs_0_
  34.7 0.2 fusion.10
  34.9 2.4 %collective-permute-start.1 = (bf16[448,1024]{1,0:T(8,128)(2,1)S(1)}, bf16[448,1024]{1,0:T(8,128)(2,1)S(1)}, u32[]{:S(2)}, u32[]{:S(2)}) collective-permute-start(bf16[448,1024]{1,0:T(8,128)(2,1)S(1)} %get-tuple-element.21), channel_id=1, source_target_pairs={{0,16},{16,0},{32,48},{48,32},{64,80},{80,64},{96,112},{112,96},{1... | collective-permute-start | bytes 2752520 | tf_op jit(solution)/shard_map/ppermute | solution.py:123
  37.3 1.9 collective-permute-start
  39.4 1.0 copy-done.1
  40.3 1.3 collective-permute-done.refs_0_
  41.7 0.9 copy-done.3
  42.6 53.1 %all-to-all-done.arrived_ref = bf16[32,16,448]{2,1,0:T(8,128)(2,1)S(1)} async-done(((bf16[32,16,448]{2,1,0:T(8,128)(2,1)}), bf16[32,16,448]{2,1,0:T(8,128)(2,1)S(1)}, u32[]{:S(2)}, u32[]{:S(2)}) %all-to-all-start) | async-done | bytes 458784 | tf_op jit(solution)/shard_map/all_to_all | solution.py:87
  95.7 0.7 partial_rows.2
  96.4 0.5 copy-done.2
  96.9 0.3 copy-done.4
  97.2 0.7 partial_rows.3
  97.9 0.2 pad_maximum_fusion
  98.1 34.1 %all_to_all.20 = bf16[16,32,2176]{2,1,0:T(8,128)(2,1)S(1)} all-to-all(bf16[16,32,2176]{2,1,0:T(8,128)(2,1)S(1)} %bitcast.29), channel_id=1, replica_groups={{0,1,2,3,4,5,6,7,8,9,10,11,12,13,14,15},{16,17,18,19,20,21,22,23,24,25,..., dimensions={0} | all-to-all | bytes 4456448 | tf_op jit(solution)/shard_map/all_to_all | solution.py:87
  132.2 0.3 convert_reduce_fusion
  132.5 0.2 fusion.9
  132.7 0.1 fusion.5
  133.0 17.6 %all_to_all.21 = bf16[16,32,1024]{2,1,0:T(8,128)(2,1)S(1)} all-to-all(bf16[16,32,1024]{2,1,0:T(8,128)(2,1)S(1)} %broadcast_in_dim.34), channel_id=1, replica_groups={{0,1,2,3,4,5,6,7,8,9,10,11,12,13,14,15},{16,17,18,19,20,21,22,23,24,25,..., dimensions={0} | all-to-all | bytes 2097152 | tf_op jit(solution)/shard_map/all_to_all | solution.py:87
  150.6 0.7 down_rows.1
  151.3 68.7 %all_to_all.22 = bf16[32,16,448]{2,1,0:T(8,128)(2,1)S(1)} all-to-all(bf16[32,16,448]{2,1,0:T(8,128)(2,1)S(1)} %down_rows.1), channel_id=1, replica_groups={{0,32,64,96,128,160,192,224,256,288,320,352,384,416,448,480,512,544,576..., dimensions={0} | all-to-all | bytes 917504 | tf_op jit(solution)/shard_map/all_to_all | solution.py:87
  220.1 1.0 convolution_convert_fusion
  (16 shorter events, 0.2 us)
Async XLA Ops:
  2.1 93.6 %all-to-all-start = ((bf16[32,16,448]{2,1,0:T(8,128)(2,1)}), bf16[32,16,448]{2,1,0:T(8,128)(2,1)S(1)}, u32[]{:S(2)}, u32[]{:S(2)}) async-start(bf16[32,16,448]{2,1,0:T(8,128)(2,1)} %bitcast.31), calls=%async_computation | async-start | bytes 1048576 | tf_op jit(solution)/shard_map/all_to_all | solution.py:87
  30.9 8.5 %collective-permute-start.2 = (bf16[1,1024,448]{1,2,0:T(8,128)(2,1)}, bf16[1,1024,448]{1,2,0:T(8,128)(2,1)S(1)}, u32[]{:S(2)}, u32[]{:S(2)}) collective-permute-start(bf16[1,1024,448]{1,2,0:T(8,128)(2,1)} %param.11), channel_id=1, source_target_pairs={{0,16},{16,0},{32,48},{48,32},{64,80},{80,64},{96,112},{112,96},{1... | collective-permute-start | bytes 2752520 | tf_op jit(solution)/shard_map/ppermute | solution.py:124
  34.7 4.5 %copy-start.5 = (bf16[128,2]{0,1:T(2,128)(2,1)S(1)}, bf16[128,2]{0,1:T(2,128)(2,1)}, u32[]{:S(2)}) copy-start(bf16[128,2]{0,1:T(2,128)(2,1)} %param.9) | copy-start | bytes 1540
  34.7 4.5 %copy-start.6 = (s32[2,128]{1,0:T(2,128)S(1)}, s32[2,128]{1,0:T(2,128)}, u32[]{:S(2)}) copy-start(s32[2,128]{1,0:T(2,128)} %get-tuple-element.14) | copy-start | bytes 3076
  34.9 4.5 %collective-permute-start.1 = (bf16[448,1024]{1,0:T(8,128)(2,1)S(1)}, bf16[448,1024]{1,0:T(8,128)(2,1)S(1)}, u32[]{:S(2)}, u32[]{:S(2)}) collective-permute-start(bf16[448,1024]{1,0:T(8,128)(2,1)S(1)} %get-tuple-element.21), channel_id=1, source_target_pairs={{0,16},{16,0},{32,48},{48,32},{64,80},{80,64},{96,112},{112,96},{1... | collective-permute-start | bytes 2752520 | tf_op jit(solution)/shard_map/ppermute | solution.py:123
  37.3 4.4 %collective-permute-start = (bf16[448,1024]{1,0:T(8,128)(2,1)S(1)}, bf16[448,1024]{1,0:T(8,128)(2,1)S(1)}, u32[]{:S(2)}, u32[]{:S(2)}) collective-permute-start(bf16[448,1024]{1,0:T(8,128)(2,1)S(1)} %get-tuple-element.22), channel_id=1, source_target_pairs={{0,16},{16,0},{32,48},{48,32},{64,80},{80,64},{96,112},{112,96},{1... | collective-permute-start | bytes 2752520 | tf_op jit(solution)/shard_map/ppermute | solution.py:122
  39.4 1.0 copy-start.1
  41.7 0.9 copy-start.3
  95.7 1.2 copy-start.2
  95.7 1.5 copy-start.4
  132.5 18.1 %copy-start = (bf16[1,1024,448]{1,2,0:T(8,128)(2,1)S(1)}, bf16[1,1024,448]{1,2,0:T(8,128)(2,1)}, u32[]{:S(2)}) copy-start(bf16[1,1024,448]{1,2,0:T(8,128)(2,1)} %param.11) | copy-start | bytes 2752516

commit v5 on v4

--- a/solution.py
+++ b/solution.py
@@ -1,4 +1,5 @@
 import functools
+import math
 
 import jax
 import jax.numpy as jnp
@@ -68,6 +69,23 @@
             done += STRIP
 
 
+def merge_rows(pieces_ref, merged_ref):
+    rows, columns = merged_ref.shape
+    both = columns - LANES
+    for start in range(0, both, STRIP):
+        strip = slice(start, start + STRIP)
+        merged_ref[:, strip] = jnp.sum(pieces_ref[:, :, strip].astype(jnp.float32), axis=0).astype(
+            jnp.bfloat16
+        )
+    tail = jnp.sum(pieces_ref[:, :, both:].astype(jnp.float32), axis=0)
+    squares = tail[:, 0:1] + tail[:, 1:2]
+    high = squares.astype(jnp.bfloat16).astype(jnp.float32)
+    column = lax.broadcasted_iota(jnp.int32, (rows, LANES), 1)
+    merged_ref[:, both:] = jnp.where(
+        column == 0, high, jnp.where(column == 1, squares - high, 0.0)
+    ).astype(jnp.bfloat16)
+
+
 def down_rows(hidden_ref, near_ref, far_ref, finished_ref):
     half = hidden_ref.shape[0] // CORES
     chips, capacity, width = finished_ref.shape
@@ -101,7 +119,18 @@
     inner = both // 2
     columns = [[CORES * chip + core for chip in range(chips)] for core in range(CORES)]
     swap = [(index, index ^ 1) for index in range(groups)]
-    every = [list(range(ways))]
+    side = math.isqrt(ways)
+    places = [
+        [
+            [group * ways + (side * b + a if group % CORES == 0 else side * a + b) for b in range(side)]
+            for a in range(side)
+        ]
+        for group in range(groups)
+    ]
+    first_lines = [[line[b] for line in part] for part in places for b in range(side)]
+    second_lines = [line for part in places for line in part]
+    planes = [[place for line in part for place in line] for part in places]
+    everywhere = ("group", "slot")
 
     rows, target = pl.pallas_call(
         functools.partial(place_rows, groups, capacity),
@@ -143,12 +172,21 @@
     sent = jnp.concatenate(
         [products(0, gained), products(1, other_gate, other_up)], axis=0
     )
-    pieces = exchange(sent.reshape(ways, slots // ways, both + LANES), "slot", every)
+    pieces = exchange(sent.reshape(side, slots // side, both + LANES), everywhere, first_lines)
+    merged = pl.pallas_call(
+        merge_rows,
+        out_shape=jax.ShapeDtypeStruct((slots // side, both + LANES), jnp.bfloat16),
+        in_specs=[whole],
+        out_specs=whole,
+        compiler_params=pltpu.CompilerParams(vmem_limit_bytes=VMEM_BYTES),
+        name="merge_rows",
+    )(pieces)
+    pieces = exchange(merged.reshape(side, slots // ways, both + LANES), everywhere, second_lines)
     mine = jnp.sum(pieces.astype(jnp.float32), axis=0)
     scale = lax.rsqrt((mine[:, both : both + 1] + mine[:, both + 1 : both + 2]) / D + NORM_EPS)
     gate, up = mine[:, :inner] * scale, mine[:, inner:both] * scale
     hidden = (jax.nn.silu(gate) * up).astype(jnp.bfloat16)
-    spread = exchange(jnp.broadcast_to(hidden[None], (ways,) + hidden.shape), "slot", every)
+    spread = exchange(jnp.broadcast_to(hidden[None], (ways,) + hidden.shape), everywhere, planes)
     finished = pl.pallas_call(
         down_rows,
         out_shape=jax.ShapeDtypeStruct((chips, CORES * capacity, width), jnp.bfloat16),

time: 222 us -> 216 us (0.973)
  blocking collectives: 121 us -> 112 us
    all_to_all x3 -> x4, blocking collectives: 121 us -> 112 us  [exchange(): lax.all_to_all(values, axis, split_axis=0, concat_axis=0, tiled=True, axi...]
where the time goes in v5:
time: 216 us; the launch traced here: 213 us
  blocking collectives  112 us (52%)
  waiting for transfers between devices  54.5 us (25%)
  starting transfers between devices  35 us (16%)
  Pallas kernels  4.72 us (2%)
  local copies, waits for them, and re-layouts  2.95 us (1%)
  other arithmetic  2.48 us (1%)
    all_to_all x4, blocking collectives, exchange(): lax.all_to_all(values, axis, split_axis=0, concat_axis=0, tiled=True, axi...  112 us
    all_to_all x1, waiting for transfers between devices, exchange(): lax.all_to_all(values, axis, split_axis=0, concat_axis=0, tiled=True, axi...  53.1 us
    all_to_all x1, starting transfers between devices, exchange(): lax.all_to_all(values, axis, split_axis=0, concat_axis=0, tiled=True, axi...  28.7 us
  transfers between devices with their start and end apart: 4, of which 2 were waited for; matrix products, arithmetic and copies ran while one was open for 1% of the time, Pallas kernels for 0%

profile of v5, /device:TPU:6, one launch (start us, length us, event | category | flops | bytes accessed | tf_op | source)
XLA Modules:
  0.0 213.1 jit_solution(7105537070277815442)
XLA Ops:
  0.0 2.1 %place_rows.1 = (bf16[512,448]{1,0:T(8,128)(2,1)}, s32[2,128]{1,0:T(2,128)}) custom-call(s32[2,128]{1,0:T(2,128)} %bitcast.36, bf16[448,128]{1,0:T(8,128)(2,1)} %bitcast.34), custom_call_target="tpu_custom_call" | custom-call | tf_op jit(solution)/shard_map/place_rows/pallas_call | solution.py:135
  2.1 28.7 %all-to-all-start = ((bf16[32,16,448]{2,1,0:T(8,128)(2,1)}), bf16[32,16,448]{2,1,0:T(8,128)(2,1)S(1)}, u32[]{:S(2)}, u32[]{:S(2)}) async-start(bf16[32,16,448]{2,1,0:T(8,128)(2,1)} %bitcast.33), calls=%async_computation | async-start | bytes 1048576 | tf_op jit(solution)/shard_map/all_to_all | solution.py:105
  30.9 1.9 collective-permute-start.2
  32.8 1.9 fusion.refs_0_
  34.7 0.2 fusion.10
  34.9 2.4 %collective-permute-start.1 = (bf16[448,1024]{1,0:T(8,128)(2,1)S(1)}, bf16[448,1024]{1,0:T(8,128)(2,1)S(1)}, u32[]{:S(2)}, u32[]{:S(2)}) collective-permute-start(bf16[448,1024]{1,0:T(8,128)(2,1)S(1)} %get-tuple-element.21), channel_id=1, source_target_pairs={{0,16},{16,0},{32,48},{48,32},{64,80},{80,64},{96,112},{112,96},{1... | collective-permute-start | bytes 2752520 | tf_op jit(solution)/shard_map/ppermute | solution.py:152
  37.3 1.9 collective-permute-start
  39.4 1.0 copy-done.1
  40.3 1.3 collective-permute-done.refs_0_
  41.7 0.9 copy-done.3
  42.6 53.1 %all-to-all-done.arrived_ref = bf16[32,16,448]{2,1,0:T(8,128)(2,1)S(1)} async-done(((bf16[32,16,448]{2,1,0:T(8,128)(2,1)}), bf16[32,16,448]{2,1,0:T(8,128)(2,1)S(1)}, u32[]{:S(2)}, u32[]{:S(2)}) %all-to-all-start) | async-done | bytes 458784 | tf_op jit(solution)/shard_map/all_to_all | solution.py:105
  95.7 0.7 partial_rows.2
  96.4 0.5 copy-done.2
  96.9 0.3 copy-done.4
  97.2 0.7 partial_rows.3
  97.9 0.2 pad_maximum_fusion
  98.1 19.7 %all_to_all.25.pieces_ref = bf16[4,128,2176]{2,1,0:T(8,128)(2,1)S(1)} all-to-all(bf16[4,128,2176]{2,1,0:T(8,128)(2,1)S(1)} %bitcast.31), channel_id=1, replica_groups={{0,1,2,3},{4,5,6,7},{8,9,10,11},{12,13,14,15},{16,20,24,28},{17,21,25,2..., dimensions={0} | all-to-all | bytes 4456448 | tf_op jit(solution)/shard_map/all_to_all | solution.py:105
  117.8 0.4 merge_rows.1
  118.2 12.5 %all_to_all.26 = bf16[4,32,2176]{2,1,0:T(8,128)(2,1)S(1)} all-to-all(bf16[4,32,2176]{2,1,0:T(8,128)(2,1)S(1)} %bitcast.28), channel_id=1, replica_groups={{0,4,8,12},{1,5,9,13},{2,6,10,14},{3,7,11,15},{16,17,18,19},{20,21,22,2..., dimensions={0} | all-to-all | bytes 1114112 | tf_op jit(solution)/shard_map/all_to_all | solution.py:105
  130.8 0.2 fusion.9
  131.3 16.6 %all_to_all.27 = bf16[16,32,1024]{2,1,0:T(8,128)(2,1)S(1)} all-to-all(bf16[16,32,1024]{2,1,0:T(8,128)(2,1)S(1)} %broadcast_in_dim.34), channel_id=1, replica_groups={{0,4,8,12,1,5,9,13,2,6,10,14,3,7,11,15},{16,17,18,19,20,21,22,23,24,25,..., dimensions={0} | all-to-all | bytes 2097152 | tf_op jit(solution)/shard_map/all_to_all | solution.py:105
  147.9 0.7 down_rows.1
  148.7 63.5 %all_to_all.28 = bf16[32,16,448]{2,1,0:T(8,128)(2,1)S(1)} all-to-all(bf16[32,16,448]{2,1,0:T(8,128)(2,1)S(1)} %down_rows.1), channel_id=1, replica_groups={{0,32,64,96,128,160,192,224,256,288,320,352,384,416,448,480,512,544,576..., dimensions={0} | all-to-all | bytes 917504 | tf_op jit(solution)/shard_map/all_to_all | solution.py:105
  212.1 1.0 convolution_convert_fusion
  (18 shorter events, 0.4 us)
Async XLA Ops:
  2.1 93.6 %all-to-all-start = ((bf16[32,16,448]{2,1,0:T(8,128)(2,1)}), bf16[32,16,448]{2,1,0:T(8,128)(2,1)S(1)}, u32[]{:S(2)}, u32[]{:S(2)}) async-start(bf16[32,16,448]{2,1,0:T(8,128)(2,1)} %bitcast.33), calls=%async_computation | async-start | bytes 1048576 | tf_op jit(solution)/shard_map/all_to_all | solution.py:105
  30.9 8.5 %collective-permute-start.2 = (bf16[1,1024,448]{1,2,0:T(8,128)(2,1)}, bf16[1,1024,448]{1,2,0:T(8,128)(2,1)S(1)}, u32[]{:S(2)}, u32[]{:S(2)}) collective-permute-start(bf16[1,1024,448]{1,2,0:T(8,128)(2,1)} %param.11), channel_id=1, source_target_pairs={{0,16},{16,0},{32,48},{48,32},{64,80},{80,64},{96,112},{112,96},{1... | collective-permute-start | bytes 2752520 | tf_op jit(solution)/shard_map/ppermute | solution.py:153
  34.7 4.5 %copy-start.5 = (bf16[128,2]{0,1:T(2,128)(2,1)S(1)}, bf16[128,2]{0,1:T(2,128)(2,1)}, u32[]{:S(2)}) copy-start(bf16[128,2]{0,1:T(2,128)(2,1)} %param.9) | copy-start | bytes 1540
  34.7 4.5 %copy-start.6 = (s32[2,128]{1,0:T(2,128)S(1)}, s32[2,128]{1,0:T(2,128)}, u32[]{:S(2)}) copy-start(s32[2,128]{1,0:T(2,128)} %get-tuple-element.14) | copy-start | bytes 3076
  34.9 4.5 %collective-permute-start.1 = (bf16[448,1024]{1,0:T(8,128)(2,1)S(1)}, bf16[448,1024]{1,0:T(8,128)(2,1)S(1)}, u32[]{:S(2)}, u32[]{:S(2)}) collective-permute-start(bf16[448,1024]{1,0:T(8,128)(2,1)S(1)} %get-tuple-element.21), channel_id=1, source_target_pairs={{0,16},{16,0},{32,48},{48,32},{64,80},{80,64},{96,112},{112,96},{1... | collective-permute-start | bytes 2752520 | tf_op jit(solution)/shard_map/ppermute | solution.py:152
  37.3 4.4 %collective-permute-start = (bf16[448,1024]{1,0:T(8,128)(2,1)S(1)}, bf16[448,1024]{1,0:T(8,128)(2,1)S(1)}, u32[]{:S(2)}, u32[]{:S(2)}) collective-permute-start(bf16[448,1024]{1,0:T(8,128)(2,1)S(1)} %get-tuple-element.22), channel_id=1, source_target_pairs={{0,16},{16,0},{32,48},{48,32},{64,80},{80,64},{96,112},{112,96},{1... | collective-permute-start | bytes 2752520 | tf_op jit(solution)/shard_map/ppermute | solution.py:151
  39.4 1.0 copy-start.1
  41.7 0.9 copy-start.3
  95.7 1.2 copy-start.2
  95.7 1.5 copy-start.4
  130.7 17.2 %copy-start = (bf16[1,1024,448]{1,2,0:T(8,128)(2,1)S(1)}, bf16[1,1024,448]{1,2,0:T(8,128)(2,1)}, u32[]{:S(2)}) copy-start(bf16[1,1024,448]{1,2,0:T(8,128)(2,1)} %param.11) | copy-start | bytes 2752516

commit v6 on v5

--- a/solution.py
+++ b/solution.py
@@ -22,7 +22,8 @@
     slots = rows_ref.shape[0]
     count = tokens_ref.shape[1]
     core = lax.rem(lax.axis_index("group"), CORES)
-    first, second = routes_ref[0:1, :] ^ core, routes_ref[1:2, :] ^ core
+    first = jnp.where(core == 0, routes_ref[0:1, :], experts - 1 - routes_ref[0:1, :])
+    second = jnp.where(core == 0, routes_ref[1:2, :], experts - 1 - routes_ref[1:2, :])
     names = lax.broadcasted_iota(jnp.int32, (experts, count), 0)
     one = (names == first).astype(jnp.float32)
     two = (names == second).astype(jnp.float32)
@@ -117,7 +118,10 @@
     slots = groups * capacity
     both = w_gate_up.shape[2]
     inner = both // 2
-    columns = [[CORES * chip + core for chip in range(chips)] for core in range(CORES)]
+    columns = [
+        [CORES * chip for chip in range(chips)],
+        [CORES * chip + 1 for chip in reversed(range(chips))],
+    ]
     swap = [(index, index ^ 1) for index in range(groups)]
     side = math.isqrt(ways)
     places = [

time: 216 us -> 214 us (level)
  the two profiles are of different devices: /device:TPU:6 before, /device:TPU:32 now
where the time goes in v6:
time: 214 us; the launch traced here: 213 us
  blocking collectives  118 us (55%)
  waiting for transfers between devices  49.4 us (23%)
  starting transfers between devices  34.9 us (16%)
  Pallas kernels  4.72 us (2%)
  local copies, waits for them, and re-layouts  2.96 us (1%)
  other arithmetic  2.48 us (1%)
    all_to_all x4, blocking collectives, exchange(): lax.all_to_all(values, axis, split_axis=0, concat_axis=0, tiled=True, axi...  118 us
    all_to_all x1, waiting for transfers between devices, exchange(): lax.all_to_all(values, axis, split_axis=0, concat_axis=0, tiled=True, axi...  48 us
    all_to_all x1, starting transfers between devices, exchange(): lax.all_to_all(values, axis, split_axis=0, concat_axis=0, tiled=True, axi...  28.6 us
  transfers between devices with their start and end apart: 4, of which 2 were waited for; matrix products, arithmetic and copies ran while one was open for 1% of the time, Pallas kernels for 0%

profile of v6, /device:TPU:32, one launch (start us, length us, event | category | flops | bytes accessed | tf_op | source)
XLA Modules:
  0.0 213.2 jit_solution(8434386594220620572)
XLA Ops:
  0.0 2.1 %place_rows.1 = (bf16[512,448]{1,0:T(8,128)(2,1)}, s32[2,128]{1,0:T(2,128)}) custom-call(s32[2,128]{1,0:T(2,128)} %bitcast.36, bf16[448,128]{1,0:T(8,128)(2,1)} %bitcast.34), custom_call_target="tpu_custom_call" | custom-call | tf_op jit(solution)/shard_map/place_rows/pallas_call | solution.py:139
  2.1 28.6 %all-to-all-start = ((bf16[32,16,448]{2,1,0:T(8,128)(2,1)}), bf16[32,16,448]{2,1,0:T(8,128)(2,1)S(1)}, u32[]{:S(2)}, u32[]{:S(2)}) async-start(bf16[32,16,448]{2,1,0:T(8,128)(2,1)} %bitcast.33), calls=%async_computation | async-start | bytes 1048576 | tf_op jit(solution)/shard_map/all_to_all | solution.py:106
  30.8 1.9 collective-permute-start.2
  32.7 1.9 fusion.refs_0_
  34.6 0.2 fusion.10
  34.7 2.4 %collective-permute-start.1 = (bf16[448,1024]{1,0:T(8,128)(2,1)S(1)}, bf16[448,1024]{1,0:T(8,128)(2,1)S(1)}, u32[]{:S(2)}, u32[]{:S(2)}) collective-permute-start(bf16[448,1024]{1,0:T(8,128)(2,1)S(1)} %get-tuple-element.21), channel_id=1, source_target_pairs={{0,16},{16,0},{32,48},{48,32},{64,80},{80,64},{96,112},{112,96},{1... | collective-permute-start | bytes 2752520 | tf_op jit(solution)/shard_map/ppermute | solution.py:156
  37.2 1.9 collective-permute-start
  39.2 1.0 copy-done.1
  40.2 1.3 collective-permute-done.refs_0_
  41.5 0.9 copy-done.3
  42.5 48.0 %all-to-all-done.arrived_ref = bf16[32,16,448]{2,1,0:T(8,128)(2,1)S(1)} async-done(((bf16[32,16,448]{2,1,0:T(8,128)(2,1)}), bf16[32,16,448]{2,1,0:T(8,128)(2,1)S(1)}, u32[]{:S(2)}, u32[]{:S(2)}) %all-to-all-start) | async-done | bytes 458784 | tf_op jit(solution)/shard_map/all_to_all | solution.py:106
  90.5 0.7 partial_rows.2
  91.2 0.5 copy-done.2
  91.7 0.3 copy-done.4
  91.9 0.7 partial_rows.3
  92.6 0.2 pad_maximum_fusion
  92.8 21.3 %all_to_all.25.pieces_ref = bf16[4,128,2176]{2,1,0:T(8,128)(2,1)S(1)} all-to-all(bf16[4,128,2176]{2,1,0:T(8,128)(2,1)S(1)} %bitcast.31), channel_id=1, replica_groups={{0,1,2,3},{4,5,6,7},{8,9,10,11},{12,13,14,15},{16,20,24,28},{17,21,25,2..., dimensions={0} | all-to-all | bytes 4456448 | tf_op jit(solution)/shard_map/all_to_all | solution.py:106
  114.1 0.4 merge_rows.1
  114.6 12.5 %all_to_all.26 = bf16[4,32,2176]{2,1,0:T(8,128)(2,1)S(1)} all-to-all(bf16[4,32,2176]{2,1,0:T(8,128)(2,1)S(1)} %bitcast.28), channel_id=1, replica_groups={{0,4,8,12},{1,5,9,13},{2,6,10,14},{3,7,11,15},{16,17,18,19},{20,21,22,2..., dimensions={0} | all-to-all | bytes 1114112 | tf_op jit(solution)/shard_map/all_to_all | solution.py:106
  127.2 0.2 fusion.9
  127.6 15.9 %all_to_all.27 = bf16[16,32,1024]{2,1,0:T(8,128)(2,1)S(1)} all-to-all(bf16[16,32,1024]{2,1,0:T(8,128)(2,1)S(1)} %broadcast_in_dim.34), channel_id=1, replica_groups={{0,4,8,12,1,5,9,13,2,6,10,14,3,7,11,15},{16,17,18,19,20,21,22,23,24,25,..., dimensions={0} | all-to-all | bytes 2097152 | tf_op jit(solution)/shard_map/all_to_all | solution.py:106
  143.5 0.7 down_rows.1
  144.2 68.0 %all_to_all.28 = bf16[32,16,448]{2,1,0:T(8,128)(2,1)S(1)} all-to-all(bf16[32,16,448]{2,1,0:T(8,128)(2,1)S(1)} %down_rows.1), channel_id=1, replica_groups={{0,32,64,96,128,160,192,224,256,288,320,352,384,416,448,480,512,544,576..., dimensions={0} | all-to-all | bytes 917504 | tf_op jit(solution)/shard_map/all_to_all | solution.py:106
  212.2 1.0 convolution_convert_fusion
  (18 shorter events, 0.4 us)
Async XLA Ops:
  2.1 88.3 %all-to-all-start = ((bf16[32,16,448]{2,1,0:T(8,128)(2,1)}), bf16[32,16,448]{2,1,0:T(8,128)(2,1)S(1)}, u32[]{:S(2)}, u32[]{:S(2)}) async-start(bf16[32,16,448]{2,1,0:T(8,128)(2,1)} %bitcast.33), calls=%async_computation | async-start | bytes 1048576 | tf_op jit(solution)/shard_map/all_to_all | solution.py:106
  30.8 8.5 %collective-permute-start.2 = (bf16[1,1024,448]{1,2,0:T(8,128)(2,1)}, bf16[1,1024,448]{1,2,0:T(8,128)(2,1)S(1)}, u32[]{:S(2)}, u32[]{:S(2)}) collective-permute-start(bf16[1,1024,448]{1,2,0:T(8,128)(2,1)} %param.11), channel_id=1, source_target_pairs={{0,16},{16,0},{32,48},{48,32},{64,80},{80,64},{96,112},{112,96},{1... | collective-permute-start | bytes 2752520 | tf_op jit(solution)/shard_map/ppermute | solution.py:157
  34.6 4.5 %copy-start.5 = (bf16[128,2]{0,1:T(2,128)(2,1)S(1)}, bf16[128,2]{0,1:T(2,128)(2,1)}, u32[]{:S(2)}) copy-start(bf16[128,2]{0,1:T(2,128)(2,1)} %param.9) | copy-start | bytes 1540
  34.6 4.5 %copy-start.6 = (s32[2,128]{1,0:T(2,128)S(1)}, s32[2,128]{1,0:T(2,128)}, u32[]{:S(2)}) copy-start(s32[2,128]{1,0:T(2,128)} %get-tuple-element.14) | copy-start | bytes 3076
  34.7 4.5 %collective-permute-start.1 = (bf16[448,1024]{1,0:T(8,128)(2,1)S(1)}, bf16[448,1024]{1,0:T(8,128)(2,1)S(1)}, u32[]{:S(2)}, u32[]{:S(2)}) collective-permute-start(bf16[448,1024]{1,0:T(8,128)(2,1)S(1)} %get-tuple-element.21), channel_id=1, source_target_pairs={{0,16},{16,0},{32,48},{48,32},{64,80},{80,64},{96,112},{112,96},{1... | collective-permute-start | bytes 2752520 | tf_op jit(solution)/shard_map/ppermute | solution.py:156
  37.2 4.4 %collective-permute-start = (bf16[448,1024]{1,0:T(8,128)(2,1)S(1)}, bf16[448,1024]{1,0:T(8,128)(2,1)S(1)}, u32[]{:S(2)}, u32[]{:S(2)}) collective-permute-start(bf16[448,1024]{1,0:T(8,128)(2,1)S(1)} %get-tuple-element.22), channel_id=1, source_target_pairs={{0,16},{16,0},{32,48},{48,32},{64,80},{80,64},{96,112},{112,96},{1... | collective-permute-start | bytes 2752520 | tf_op jit(solution)/shard_map/ppermute | solution.py:155
  39.2 1.0 copy-start.1
  41.5 0.9 copy-start.3
  90.5 1.2 copy-start.2
  90.5 1.5 copy-start.4
  127.1 16.4 %copy-start = (bf16[1,1024,448]{1,2,0:T(8,128)(2,1)S(1)}, bf16[1,1024,448]{1,2,0:T(8,128)(2,1)}, u32[]{:S(2)}) copy-start(bf16[1,1024,448]{1,2,0:T(8,128)(2,1)} %param.11) | copy-start | bytes 2752516

commit v7 on v6

--- a/solution.py
+++ b/solution.py
@@ -14,6 +14,7 @@
 NORM_EPS = 1e-06
 LANES = 128
 STRIP = 512
+STEP = 5
 VMEM_BYTES = 32 * 1024 * 1024
 CORES = 2
 
@@ -21,9 +22,13 @@
 def place_rows(experts, capacity, routes_ref, tokens_ref, rows_ref, target_ref):
     slots = rows_ref.shape[0]
     count = tokens_ref.shape[1]
+    chips = experts // CORES
+    back = pow(STEP, -1, chips)
     core = lax.rem(lax.axis_index("group"), CORES)
-    first = jnp.where(core == 0, routes_ref[0:1, :], experts - 1 - routes_ref[0:1, :])
-    second = jnp.where(core == 0, routes_ref[1:2, :], experts - 1 - routes_ref[1:2, :])
+    chosen = routes_ref[...]
+    chosen = CORES * (((chosen >> 1) * back) & (chips - 1)) + (chosen & 1)
+    chosen = jnp.where(core == 0, chosen, experts - 1 - chosen)
+    first, second = chosen[0:1, :], chosen[1:2, :]
     names = lax.broadcasted_iota(jnp.int32, (experts, count), 0)
     one = (names == first).astype(jnp.float32)
     two = (names == second).astype(jnp.float32)
@@ -118,9 +123,10 @@
     slots = groups * capacity
     both = w_gate_up.shape[2]
     inner = both // 2
+    listed = [STEP * place % chips for place in range(chips)]
     columns = [
-        [CORES * chip for chip in range(chips)],
-        [CORES * chip + 1 for chip in reversed(range(chips))],
+        [CORES * chip for chip in listed],
+        [CORES * chip + 1 for chip in reversed(listed)],
     ]
     swap = [(index, index ^ 1) for index in range(groups)]
     side = math.isqrt(ways)

time: 214 us -> 209 us (0.977)
  blocking collectives: 118 us -> 115 us
  waiting for transfers between devices: 49.4 us -> 46.8 us
    all_to_all x1, waiting for transfers between devices: 48 us -> 45.4 us  [exchange(): lax.all_to_all(values, axis, split_axis=0, concat_axis=0, tiled=True, axi...]
    all_to_all x4, blocking collectives: 118 us -> 115 us  [exchange(): lax.all_to_all(values, axis, split_axis=0, concat_axis=0, tiled=True, axi...]
where the time goes in v7:
time: 209 us; the launch traced here: 208 us
  blocking collectives  115 us (55%)
  waiting for transfers between devices  46.8 us (22%)
  starting transfers between devices  34.9 us (17%)
  Pallas kernels  4.72 us (2%)
  local copies, waits for them, and re-layouts  2.96 us (1%)
  other arithmetic  2.48 us (1%)
    all_to_all x4, blocking collectives, exchange(): lax.all_to_all(values, axis, split_axis=0, concat_axis=0, tiled=True, axi...  115 us
    all_to_all x1, waiting for transfers between devices, exchange(): lax.all_to_all(values, axis, split_axis=0, concat_axis=0, tiled=True, axi...  45.4 us
    all_to_all x1, starting transfers between devices, exchange(): lax.all_to_all(values, axis, split_axis=0, concat_axis=0, tiled=True, axi...  28.6 us
  transfers between devices with their start and end apart: 4, of which 2 were waited for; matrix products, arithmetic and copies ran while one was open for 1% of the time, Pallas kernels for 0%

profile of v7, /device:TPU:32, one launch (start us, length us, event | category | flops | bytes accessed | tf_op | source)
XLA Modules:
  0.0 208.2 jit_solution(15519790101480151703)
XLA Ops:
  0.0 2.1 %place_rows.1 = (bf16[512,448]{1,0:T(8,128)(2,1)}, s32[2,128]{1,0:T(2,128)}) custom-call(s32[2,128]{1,0:T(2,128)} %bitcast.36, bf16[448,128]{1,0:T(8,128)(2,1)} %bitcast.34), custom_call_target="tpu_custom_call" | custom-call | tf_op jit(solution)/shard_map/place_rows/pallas_call | solution.py:145
  2.1 28.6 %all-to-all-start = ((bf16[32,16,448]{2,1,0:T(8,128)(2,1)}), bf16[32,16,448]{2,1,0:T(8,128)(2,1)S(1)}, u32[]{:S(2)}, u32[]{:S(2)}) async-start(bf16[32,16,448]{2,1,0:T(8,128)(2,1)} %bitcast.33), calls=%async_computation | async-start | bytes 1048576 | tf_op jit(solution)/shard_map/all_to_all | solution.py:111
  30.8 1.9 collective-permute-start.2
  32.7 1.9 fusion.refs_0_
  34.6 0.2 fusion.10
  34.7 2.4 %collective-permute-start.1 = (bf16[448,1024]{1,0:T(8,128)(2,1)S(1)}, bf16[448,1024]{1,0:T(8,128)(2,1)S(1)}, u32[]{:S(2)}, u32[]{:S(2)}) collective-permute-start(bf16[448,1024]{1,0:T(8,128)(2,1)S(1)} %get-tuple-element.21), channel_id=1, source_target_pairs={{0,16},{16,0},{32,48},{48,32},{64,80},{80,64},{96,112},{112,96},{1... | collective-permute-start | bytes 2752520 | tf_op jit(solution)/shard_map/ppermute | solution.py:162
  37.2 1.9 collective-permute-start
  39.2 1.0 copy-done.1
  40.2 1.3 collective-permute-done.refs_0_
  41.5 0.9 copy-done.3
  42.5 45.4 %all-to-all-done.arrived_ref = bf16[32,16,448]{2,1,0:T(8,128)(2,1)S(1)} async-done(((bf16[32,16,448]{2,1,0:T(8,128)(2,1)}), bf16[32,16,448]{2,1,0:T(8,128)(2,1)S(1)}, u32[]{:S(2)}, u32[]{:S(2)}) %all-to-all-start) | async-done | bytes 458784 | tf_op jit(solution)/shard_map/all_to_all | solution.py:111
  87.9 0.7 partial_rows.2
  88.6 0.5 copy-done.2
  89.1 0.3 copy-done.4
  89.3 0.7 partial_rows.3
  90.1 0.2 pad_maximum_fusion
  90.2 21.3 %all_to_all.25.pieces_ref = bf16[4,128,2176]{2,1,0:T(8,128)(2,1)S(1)} all-to-all(bf16[4,128,2176]{2,1,0:T(8,128)(2,1)S(1)} %bitcast.31), channel_id=1, replica_groups={{0,1,2,3},{4,5,6,7},{8,9,10,11},{12,13,14,15},{16,20,24,28},{17,21,25,2..., dimensions={0} | all-to-all | bytes 4456448 | tf_op jit(solution)/shard_map/all_to_all | solution.py:111
  111.5 0.4 merge_rows.1
  112.0 18.7 %all_to_all.26 = bf16[4,32,2176]{2,1,0:T(8,128)(2,1)S(1)} all-to-all(bf16[4,32,2176]{2,1,0:T(8,128)(2,1)S(1)} %bitcast.28), channel_id=1, replica_groups={{0,4,8,12},{1,5,9,13},{2,6,10,14},{3,7,11,15},{16,17,18,19},{20,21,22,2..., dimensions={0} | all-to-all | bytes 1114112 | tf_op jit(solution)/shard_map/all_to_all | solution.py:111
  130.7 0.2 fusion.9
  131.2 15.6 %all_to_all.27 = bf16[16,32,1024]{2,1,0:T(8,128)(2,1)S(1)} all-to-all(bf16[16,32,1024]{2,1,0:T(8,128)(2,1)S(1)} %broadcast_in_dim.34), channel_id=1, replica_groups={{0,4,8,12,1,5,9,13,2,6,10,14,3,7,11,15},{16,17,18,19,20,21,22,23,24,25,..., dimensions={0} | all-to-all | bytes 2097152 | tf_op jit(solution)/shard_map/all_to_all | solution.py:111
  146.8 0.7 down_rows.1
  147.5 59.7 %all_to_all.28 = bf16[32,16,448]{2,1,0:T(8,128)(2,1)S(1)} all-to-all(bf16[32,16,448]{2,1,0:T(8,128)(2,1)S(1)} %down_rows.1), channel_id=1, replica_groups={{0,160,320,480,640,800,960,96,256,416,576,736,896,32,192,352,512,672,83..., dimensions={0} | all-to-all | bytes 917504 | tf_op jit(solution)/shard_map/all_to_all | solution.py:111
  207.2 1.0 convolution_convert_fusion
  (18 shorter events, 0.4 us)
Async XLA Ops:
  2.1 85.7 %all-to-all-start = ((bf16[32,16,448]{2,1,0:T(8,128)(2,1)}), bf16[32,16,448]{2,1,0:T(8,128)(2,1)S(1)}, u32[]{:S(2)}, u32[]{:S(2)}) async-start(bf16[32,16,448]{2,1,0:T(8,128)(2,1)} %bitcast.33), calls=%async_computation | async-start | bytes 1048576 | tf_op jit(solution)/shard_map/all_to_all | solution.py:111
  30.8 8.5 %collective-permute-start.2 = (bf16[1,1024,448]{1,2,0:T(8,128)(2,1)}, bf16[1,1024,448]{1,2,0:T(8,128)(2,1)S(1)}, u32[]{:S(2)}, u32[]{:S(2)}) collective-permute-start(bf16[1,1024,448]{1,2,0:T(8,128)(2,1)} %param.11), channel_id=1, source_target_pairs={{0,16},{16,0},{32,48},{48,32},{64,80},{80,64},{96,112},{112,96},{1... | collective-permute-start | bytes 2752520 | tf_op jit(solution)/shard_map/ppermute | solution.py:163
  34.6 4.5 %copy-start.5 = (bf16[128,2]{0,1:T(2,128)(2,1)S(1)}, bf16[128,2]{0,1:T(2,128)(2,1)}, u32[]{:S(2)}) copy-start(bf16[128,2]{0,1:T(2,128)(2,1)} %param.9) | copy-start | bytes 1540
  34.6 4.5 %copy-start.6 = (s32[2,128]{1,0:T(2,128)S(1)}, s32[2,128]{1,0:T(2,128)}, u32[]{:S(2)}) copy-start(s32[2,128]{1,0:T(2,128)} %get-tuple-element.14) | copy-start | bytes 3076
  34.7 4.5 %collective-permute-start.1 = (bf16[448,1024]{1,0:T(8,128)(2,1)S(1)}, bf16[448,1024]{1,0:T(8,128)(2,1)S(1)}, u32[]{:S(2)}, u32[]{:S(2)}) collective-permute-start(bf16[448,1024]{1,0:T(8,128)(2,1)S(1)} %get-tuple-element.21), channel_id=1, source_target_pairs={{0,16},{16,0},{32,48},{48,32},{64,80},{80,64},{96,112},{112,96},{1... | collective-permute-start | bytes 2752520 | tf_op jit(solution)/shard_map/ppermute | solution.py:162
  37.2 4.4 %collective-permute-start = (bf16[448,1024]{1,0:T(8,128)(2,1)S(1)}, bf16[448,1024]{1,0:T(8,128)(2,1)S(1)}, u32[]{:S(2)}, u32[]{:S(2)}) collective-permute-start(bf16[448,1024]{1,0:T(8,128)(2,1)S(1)} %get-tuple-element.22), channel_id=1, source_target_pairs={{0,16},{16,0},{32,48},{48,32},{64,80},{80,64},{96,112},{112,96},{1... | collective-permute-start | bytes 2752520 | tf_op jit(solution)/shard_map/ppermute | solution.py:161
  39.2 1.0 copy-start.1
  41.5 0.9 copy-start.3
  87.9 1.2 copy-start.2
  87.9 1.5 copy-start.4
  130.7 16.1 %copy-start = (bf16[1,1024,448]{1,2,0:T(8,128)(2,1)S(1)}, bf16[1,1024,448]{1,2,0:T(8,128)(2,1)}, u32[]{:S(2)}) copy-start(bf16[1,1024,448]{1,2,0:T(8,128)(2,1)} %param.11) | copy-start | bytes 2752516

commit v8 on v7

--- a/solution.py
+++ b/solution.py
@@ -14,7 +14,7 @@
 NORM_EPS = 1e-06
 LANES = 128
 STRIP = 512
-STEP = 5
+STEP = 15
 VMEM_BYTES = 32 * 1024 * 1024
 CORES = 2
 

time: 209 us -> 203 us (0.971)
  the two profiles are of different devices: /device:TPU:32 before, /device:TPU:6 now
where the time goes in v8:
time: 203 us; the launch traced here: 201 us
  blocking collectives  113 us (56%)
  starting transfers between devices  40.6 us (20%)
  waiting for transfers between devices  35.9 us (18%)
  Pallas kernels  4.72 us (2%)
  local copies, waits for them, and re-layouts  2.95 us (1%)
  other arithmetic  2.48 us (1%)
    all_to_all x4, blocking collectives, exchange(): lax.all_to_all(values, axis, split_axis=0, concat_axis=0, tiled=True, axi...  113 us
    all_to_all x1, waiting for transfers between devices, exchange(): lax.all_to_all(values, axis, split_axis=0, concat_axis=0, tiled=True, axi...  35 us
    all_to_all x1, starting transfers between devices, exchange(): lax.all_to_all(values, axis, split_axis=0, concat_axis=0, tiled=True, axi...  28.7 us
    ppermute x1, starting transfers between devices, local(): other_down = lax.ppermute(w_down, 'group', swap)  7.53 us
  transfers between devices with their start and end apart: 4, of which 2 were waited for; matrix products, arithmetic and copies ran while one was open for 1% of the time, Pallas kernels for 0%

profile of v8, /device:TPU:6, one launch (start us, length us, event | category | flops | bytes accessed | tf_op | source)
XLA Modules:
  0.0 201.3 jit_solution(7131391390947359288)
XLA Ops:
  0.0 2.1 %place_rows.1 = (bf16[512,448]{1,0:T(8,128)(2,1)}, s32[2,128]{1,0:T(2,128)}) custom-call(s32[2,128]{1,0:T(2,128)} %bitcast.36, bf16[448,128]{1,0:T(8,128)(2,1)} %bitcast.34), custom_call_target="tpu_custom_call" | custom-call | tf_op jit(solution)/shard_map/place_rows/pallas_call | solution.py:145
  2.1 28.7 %all-to-all-start = ((bf16[32,16,448]{2,1,0:T(8,128)(2,1)}), bf16[32,16,448]{2,1,0:T(8,128)(2,1)S(1)}, u32[]{:S(2)}, u32[]{:S(2)}) async-start(bf16[32,16,448]{2,1,0:T(8,128)(2,1)} %bitcast.33), calls=%async_computation | async-start | bytes 1048576 | tf_op jit(solution)/shard_map/all_to_all | solution.py:111
  30.9 7.5 %collective-permute-start.2 = (bf16[1,1024,448]{1,2,0:T(8,128)(2,1)}, bf16[1,1024,448]{1,2,0:T(8,128)(2,1)S(1)}, u32[]{:S(2)}, u32[]{:S(2)}) collective-permute-start(bf16[1,1024,448]{1,2,0:T(8,128)(2,1)} %param.11), channel_id=1, source_target_pairs={{0,16},{16,0},{32,48},{48,32},{64,80},{80,64},{96,112},{112,96},{1... | collective-permute-start | bytes 2752520 | tf_op jit(solution)/shard_map/ppermute | solution.py:163
  38.4 1.9 fusion.refs_0_
  40.3 0.2 fusion.10
  40.5 1.9 collective-permute-start.1
  42.4 2.4 %collective-permute-start = (bf16[448,1024]{1,0:T(8,128)(2,1)S(1)}, bf16[448,1024]{1,0:T(8,128)(2,1)S(1)}, u32[]{:S(2)}, u32[]{:S(2)}) collective-permute-start(bf16[448,1024]{1,0:T(8,128)(2,1)S(1)} %get-tuple-element.22), channel_id=1, source_target_pairs={{0,16},{16,0},{32,48},{48,32},{64,80},{80,64},{96,112},{112,96},{1... | collective-permute-start | bytes 2752520 | tf_op jit(solution)/shard_map/ppermute | solution.py:161
  45.0 1.0 copy-done.1
  45.9 1.0 collective-permute-done.refs_0_
  46.9 0.9 copy-done.3
  47.8 35.0 %all-to-all-done.arrived_ref = bf16[32,16,448]{2,1,0:T(8,128)(2,1)S(1)} async-done(((bf16[32,16,448]{2,1,0:T(8,128)(2,1)}), bf16[32,16,448]{2,1,0:T(8,128)(2,1)S(1)}, u32[]{:S(2)}, u32[]{:S(2)}) %all-to-all-start) | async-done | bytes 458784 | tf_op jit(solution)/shard_map/all_to_all | solution.py:111
  82.8 0.7 partial_rows.2
  83.5 0.5 copy-done.2
  84.0 0.3 copy-done.4
  84.2 0.7 partial_rows.3
  85.0 0.2 pad_maximum_fusion
  85.1 19.7 %all_to_all.25.pieces_ref = bf16[4,128,2176]{2,1,0:T(8,128)(2,1)S(1)} all-to-all(bf16[4,128,2176]{2,1,0:T(8,128)(2,1)S(1)} %bitcast.31), channel_id=1, replica_groups={{0,1,2,3},{4,5,6,7},{8,9,10,11},{12,13,14,15},{16,20,24,28},{17,21,25,2..., dimensions={0} | all-to-all | bytes 4456448 | tf_op jit(solution)/shard_map/all_to_all | solution.py:111
  104.8 0.4 merge_rows.1
  105.3 12.5 %all_to_all.26 = bf16[4,32,2176]{2,1,0:T(8,128)(2,1)S(1)} all-to-all(bf16[4,32,2176]{2,1,0:T(8,128)(2,1)S(1)} %bitcast.28), channel_id=1, replica_groups={{0,4,8,12},{1,5,9,13},{2,6,10,14},{3,7,11,15},{16,17,18,19},{20,21,22,2..., dimensions={0} | all-to-all | bytes 1114112 | tf_op jit(solution)/shard_map/all_to_all | solution.py:111
  117.9 0.2 fusion.9
  118.3 15.9 %all_to_all.27 = bf16[16,32,1024]{2,1,0:T(8,128)(2,1)S(1)} all-to-all(bf16[16,32,1024]{2,1,0:T(8,128)(2,1)S(1)} %broadcast_in_dim.34), channel_id=1, replica_groups={{0,4,8,12,1,5,9,13,2,6,10,14,3,7,11,15},{16,17,18,19,20,21,22,23,24,25,..., dimensions={0} | all-to-all | bytes 2097152 | tf_op jit(solution)/shard_map/all_to_all | solution.py:111
  134.2 0.7 down_rows.1
  135.0 65.3 %all_to_all.28 = bf16[32,16,448]{2,1,0:T(8,128)(2,1)S(1)} all-to-all(bf16[32,16,448]{2,1,0:T(8,128)(2,1)S(1)} %down_rows.1), channel_id=1, replica_groups={{0,480,960,416,896,352,832,288,768,224,704,160,640,96,576,32,512,992,44..., dimensions={0} | all-to-all | bytes 917504 | tf_op jit(solution)/shard_map/all_to_all | solution.py:111
  200.3 1.0 convolution_convert_fusion
  (18 shorter events, 0.4 us)
Async XLA Ops:
  2.1 80.7 %all-to-all-start = ((bf16[32,16,448]{2,1,0:T(8,128)(2,1)}), bf16[32,16,448]{2,1,0:T(8,128)(2,1)S(1)}, u32[]{:S(2)}, u32[]{:S(2)}) async-start(bf16[32,16,448]{2,1,0:T(8,128)(2,1)} %bitcast.33), calls=%async_computation | async-start | bytes 1048576 | tf_op jit(solution)/shard_map/all_to_all | solution.py:111
  30.9 14.1 %collective-permute-start.2 = (bf16[1,1024,448]{1,2,0:T(8,128)(2,1)}, bf16[1,1024,448]{1,2,0:T(8,128)(2,1)S(1)}, u32[]{:S(2)}, u32[]{:S(2)}) collective-permute-start(bf16[1,1024,448]{1,2,0:T(8,128)(2,1)} %param.11), channel_id=1, source_target_pairs={{0,16},{16,0},{32,48},{48,32},{64,80},{80,64},{96,112},{112,96},{1... | collective-permute-start | bytes 2752520 | tf_op jit(solution)/shard_map/ppermute | solution.py:163
  40.3 4.5 %copy-start.5 = (bf16[128,2]{0,1:T(2,128)(2,1)S(1)}, bf16[128,2]{0,1:T(2,128)(2,1)}, u32[]{:S(2)}) copy-start(bf16[128,2]{0,1:T(2,128)(2,1)} %param.9) | copy-start | bytes 1540
  40.3 4.5 %copy-start.6 = (s32[2,128]{1,0:T(2,128)S(1)}, s32[2,128]{1,0:T(2,128)}, u32[]{:S(2)}) copy-start(s32[2,128]{1,0:T(2,128)} %get-tuple-element.14) | copy-start | bytes 3076
  40.5 4.5 %collective-permute-start.1 = (bf16[448,1024]{1,0:T(8,128)(2,1)S(1)}, bf16[448,1024]{1,0:T(8,128)(2,1)S(1)}, u32[]{:S(2)}, u32[]{:S(2)}) collective-permute-start(bf16[448,1024]{1,0:T(8,128)(2,1)S(1)} %get-tuple-element.21), channel_id=1, source_target_pairs={{0,16},{16,0},{32,48},{48,32},{64,80},{80,64},{96,112},{112,96},{1... | collective-permute-start | bytes 2752520 | tf_op jit(solution)/shard_map/ppermute | solution.py:162
  42.4 4.5 %collective-permute-start = (bf16[448,1024]{1,0:T(8,128)(2,1)S(1)}, bf16[448,1024]{1,0:T(8,128)(2,1)S(1)}, u32[]{:S(2)}, u32[]{:S(2)}) collective-permute-start(bf16[448,1024]{1,0:T(8,128)(2,1)S(1)} %get-tuple-element.22), channel_id=1, source_target_pairs={{0,16},{16,0},{32,48},{48,32},{64,80},{80,64},{96,112},{112,96},{1... | collective-permute-start | bytes 2752520 | tf_op jit(solution)/shard_map/ppermute | solution.py:161
  45.0 1.0 copy-start.1
  46.9 0.9 copy-start.3
  82.8 1.2 copy-start.2
  82.8 1.5 copy-start.4
  117.8 16.4 %copy-start = (bf16[1,1024,448]{1,2,0:T(8,128)(2,1)S(1)}, bf16[1,1024,448]{1,2,0:T(8,128)(2,1)}, u32[]{:S(2)}) copy-start(bf16[1,1024,448]{1,2,0:T(8,128)(2,1)} %param.11) | copy-start | bytes 2752516

commit v9 on v8

--- a/solution.py
+++ b/solution.py
@@ -132,7 +132,7 @@
     side = math.isqrt(ways)
     places = [
         [
-            [group * ways + (side * b + a if group % CORES == 0 else side * a + b) for b in range(side)]
+            [group * ways + (side * b + a if group % CORES == 0 else ways - 1 - side * a - b) for b in range(side)]
             for a in range(side)
         ]
         for group in range(groups)

time: 203 us -> 203 us (level)
  no operation moved by 1% of the time
where the time goes in v9:
time: 203 us; the launch traced here: 202 us
  blocking collectives  114 us (56%)
  starting transfers between devices  40.6 us (20%)
  waiting for transfers between devices  35.9 us (18%)
  Pallas kernels  4.72 us (2%)
  local copies, waits for them, and re-layouts  2.95 us (1%)
  other arithmetic  2.48 us (1%)
    all_to_all x4, blocking collectives, exchange(): lax.all_to_all(values, axis, split_axis=0, concat_axis=0, tiled=True, axi...  114 us
    all_to_all x1, waiting for transfers between devices, exchange(): lax.all_to_all(values, axis, split_axis=0, concat_axis=0, tiled=True, axi...  35 us
    all_to_all x1, starting transfers between devices, exchange(): lax.all_to_all(values, axis, split_axis=0, concat_axis=0, tiled=True, axi...  28.7 us
    ppermute x1, starting transfers between devices, local(): other_down = lax.ppermute(w_down, 'group', swap)  7.53 us
  transfers between devices with their start and end apart: 4, of which 2 were waited for; matrix products, arithmetic and copies ran while one was open for 1% of the time, Pallas kernels for 0%

profile of v9, /device:TPU:6, one launch (start us, length us, event | category | flops | bytes accessed | tf_op | source)
XLA Modules:
  0.0 202.0 jit_solution(17700860524873523308)
XLA Ops:
  0.0 2.1 %place_rows.1 = (bf16[512,448]{1,0:T(8,128)(2,1)}, s32[2,128]{1,0:T(2,128)}) custom-call(s32[2,128]{1,0:T(2,128)} %bitcast.36, bf16[448,128]{1,0:T(8,128)(2,1)} %bitcast.34), custom_call_target="tpu_custom_call" | custom-call | tf_op jit(solution)/shard_map/place_rows/pallas_call | solution.py:145
  2.1 28.7 %all-to-all-start = ((bf16[32,16,448]{2,1,0:T(8,128)(2,1)}), bf16[32,16,448]{2,1,0:T(8,128)(2,1)S(1)}, u32[]{:S(2)}, u32[]{:S(2)}) async-start(bf16[32,16,448]{2,1,0:T(8,128)(2,1)} %bitcast.33), calls=%async_computation | async-start | bytes 1048576 | tf_op jit(solution)/shard_map/all_to_all | solution.py:111
  30.9 7.5 %collective-permute-start.2 = (bf16[1,1024,448]{1,2,0:T(8,128)(2,1)}, bf16[1,1024,448]{1,2,0:T(8,128)(2,1)S(1)}, u32[]{:S(2)}, u32[]{:S(2)}) collective-permute-start(bf16[1,1024,448]{1,2,0:T(8,128)(2,1)} %param.11), channel_id=1, source_target_pairs={{0,16},{16,0},{32,48},{48,32},{64,80},{80,64},{96,112},{112,96},{1... | collective-permute-start | bytes 2752520 | tf_op jit(solution)/shard_map/ppermute | solution.py:163
  38.4 1.9 fusion.refs_0_
  40.3 0.2 fusion.10
  40.5 1.9 collective-permute-start.1
  42.4 2.4 %collective-permute-start = (bf16[448,1024]{1,0:T(8,128)(2,1)S(1)}, bf16[448,1024]{1,0:T(8,128)(2,1)S(1)}, u32[]{:S(2)}, u32[]{:S(2)}) collective-permute-start(bf16[448,1024]{1,0:T(8,128)(2,1)S(1)} %get-tuple-element.22), channel_id=1, source_target_pairs={{0,16},{16,0},{32,48},{48,32},{64,80},{80,64},{96,112},{112,96},{1... | collective-permute-start | bytes 2752520 | tf_op jit(solution)/shard_map/ppermute | solution.py:161
  45.0 1.0 copy-done.1
  45.9 1.0 collective-permute-done.refs_0_
  46.9 0.9 copy-done.3
  47.8 35.0 %all-to-all-done.arrived_ref = bf16[32,16,448]{2,1,0:T(8,128)(2,1)S(1)} async-done(((bf16[32,16,448]{2,1,0:T(8,128)(2,1)}), bf16[32,16,448]{2,1,0:T(8,128)(2,1)S(1)}, u32[]{:S(2)}, u32[]{:S(2)}) %all-to-all-start) | async-done | bytes 458784 | tf_op jit(solution)/shard_map/all_to_all | solution.py:111
  82.8 0.7 partial_rows.2
  83.5 0.5 copy-done.2
  84.0 0.3 copy-done.4
  84.2 0.7 partial_rows.3
  85.0 0.2 pad_maximum_fusion
  85.1 19.7 %all_to_all.25.pieces_ref = bf16[4,128,2176]{2,1,0:T(8,128)(2,1)S(1)} all-to-all(bf16[4,128,2176]{2,1,0:T(8,128)(2,1)S(1)} %bitcast.31), channel_id=1, replica_groups={{0,1,2,3},{4,5,6,7},{8,9,10,11},{12,13,14,15},{31,27,23,19},{30,26,22,1..., dimensions={0} | all-to-all | bytes 4456448 | tf_op jit(solution)/shard_map/all_to_all | solution.py:111
  104.8 0.4 merge_rows.1
  105.3 12.5 %all_to_all.26 = bf16[4,32,2176]{2,1,0:T(8,128)(2,1)S(1)} all-to-all(bf16[4,32,2176]{2,1,0:T(8,128)(2,1)S(1)} %bitcast.28), channel_id=1, replica_groups={{0,4,8,12},{1,5,9,13},{2,6,10,14},{3,7,11,15},{31,30,29,28},{27,26,25,2..., dimensions={0} | all-to-all | bytes 1114112 | tf_op jit(solution)/shard_map/all_to_all | solution.py:111
  117.9 0.2 fusion.9
  118.3 15.8 %all_to_all.27 = bf16[16,32,1024]{2,1,0:T(8,128)(2,1)S(1)} all-to-all(bf16[16,32,1024]{2,1,0:T(8,128)(2,1)S(1)} %broadcast_in_dim.34), channel_id=1, replica_groups={{0,4,8,12,1,5,9,13,2,6,10,14,3,7,11,15},{31,30,29,28,27,26,25,24,23,22,..., dimensions={0} | all-to-all | bytes 2097152 | tf_op jit(solution)/shard_map/all_to_all | solution.py:111
  134.2 0.7 down_rows.1
  134.9 66.1 %all_to_all.28 = bf16[32,16,448]{2,1,0:T(8,128)(2,1)S(1)} all-to-all(bf16[32,16,448]{2,1,0:T(8,128)(2,1)S(1)} %down_rows.1), channel_id=1, replica_groups={{0,480,960,416,896,352,832,288,768,224,704,160,640,96,576,32,512,992,44..., dimensions={0} | all-to-all | bytes 917504 | tf_op jit(solution)/shard_map/all_to_all | solution.py:111
  201.0 1.0 convolution_convert_fusion
  (18 shorter events, 0.4 us)
Async XLA Ops:
  2.1 80.7 %all-to-all-start = ((bf16[32,16,448]{2,1,0:T(8,128)(2,1)}), bf16[32,16,448]{2,1,0:T(8,128)(2,1)S(1)}, u32[]{:S(2)}, u32[]{:S(2)}) async-start(bf16[32,16,448]{2,1,0:T(8,128)(2,1)} %bitcast.33), calls=%async_computation | async-start | bytes 1048576 | tf_op jit(solution)/shard_map/all_to_all | solution.py:111
  30.9 14.1 %collective-permute-start.2 = (bf16[1,1024,448]{1,2,0:T(8,128)(2,1)}, bf16[1,1024,448]{1,2,0:T(8,128)(2,1)S(1)}, u32[]{:S(2)}, u32[]{:S(2)}) collective-permute-start(bf16[1,1024,448]{1,2,0:T(8,128)(2,1)} %param.11), channel_id=1, source_target_pairs={{0,16},{16,0},{32,48},{48,32},{64,80},{80,64},{96,112},{112,96},{1... | collective-permute-start | bytes 2752520 | tf_op jit(solution)/shard_map/ppermute | solution.py:163
  40.3 4.5 %copy-start.5 = (bf16[128,2]{0,1:T(2,128)(2,1)S(1)}, bf16[128,2]{0,1:T(2,128)(2,1)}, u32[]{:S(2)}) copy-start(bf16[128,2]{0,1:T(2,128)(2,1)} %param.9) | copy-start | bytes 1540
  40.3 4.5 %copy-start.6 = (s32[2,128]{1,0:T(2,128)S(1)}, s32[2,128]{1,0:T(2,128)}, u32[]{:S(2)}) copy-start(s32[2,128]{1,0:T(2,128)} %get-tuple-element.14) | copy-start | bytes 3076
  40.5 4.5 %collective-permute-start.1 = (bf16[448,1024]{1,0:T(8,128)(2,1)S(1)}, bf16[448,1024]{1,0:T(8,128)(2,1)S(1)}, u32[]{:S(2)}, u32[]{:S(2)}) collective-permute-start(bf16[448,1024]{1,0:T(8,128)(2,1)S(1)} %get-tuple-element.21), channel_id=1, source_target_pairs={{0,16},{16,0},{32,48},{48,32},{64,80},{80,64},{96,112},{112,96},{1... | collective-permute-start | bytes 2752520 | tf_op jit(solution)/shard_map/ppermute | solution.py:162
  42.4 4.5 %collective-permute-start = (bf16[448,1024]{1,0:T(8,128)(2,1)S(1)}, bf16[448,1024]{1,0:T(8,128)(2,1)S(1)}, u32[]{:S(2)}, u32[]{:S(2)}) collective-permute-start(bf16[448,1024]{1,0:T(8,128)(2,1)S(1)} %get-tuple-element.22), channel_id=1, source_target_pairs={{0,16},{16,0},{32,48},{48,32},{64,80},{80,64},{96,112},{112,96},{1... | collective-permute-start | bytes 2752520 | tf_op jit(solution)/shard_map/ppermute | solution.py:161
  45.0 1.0 copy-start.1
  46.9 0.9 copy-start.3
  82.8 1.2 copy-start.2
  82.8 1.5 copy-start.4
  117.8 16.4 %copy-start = (bf16[1,1024,448]{1,2,0:T(8,128)(2,1)S(1)}, bf16[1,1024,448]{1,2,0:T(8,128)(2,1)}, u32[]{:S(2)}) copy-start(bf16[1,1024,448]{1,2,0:T(8,128)(2,1)} %param.11) | copy-start | bytes 2752516
